TPU v7x, 128 devices: a whole 4x4x4 slice. The times are simulated.
128 devices in a mesh: pipe: 8 (over z, y_lo), expert: 16 (over x, y_hi, core).
Axes of the slice: x: 4, y: 4 (y_hi: 2, y_lo: 2; y = y_hi * 2 + y_lo), z: 4, core: 2. Of those that a mesh axis runs over, the one named last changes fastest.
Arguments:
- stream: bfloat16 [2, 256, 3584], P(None, 'expert', 'pipe'), may hold values from -6 to 6
- layer_gain: float32 [8, 3584], P('pipe'), may hold values from 0.5 to 1.5
- router_weight: bfloat16 [8, 3584, 16], P('pipe'), may hold values from -0.09375 to 0.09375
- gate_weight: bfloat16 [8, 16, 3584, 1024], P('pipe', 'expert'), may hold values from -0.09375 to 0.09375
- up_weight: bfloat16 [8, 16, 3584, 1024], P('pipe', 'expert'), may hold values from -0.09375 to 0.09375
- down_weight: bfloat16 [8, 16, 1024, 3584], P('pipe', 'expert'), may hold values from -0.1875 to 0.1875
- routes: int32 [8, 2, 256, 8], P('pipe', None, 'expert'), may hold values from 0 to 15, all different within a row; in each aligned block of 16 rows (0 to 15, 16 to 31, ..., all dimensions but the last counted through in order) at most 8 rows name the same one
- final_gain: float32 [3584], replicated, may hold values from 0.5 to 1.5
- head_weight: bfloat16 [65536, 3584], P(('pipe', 'expert'))
- targets: int32 [2, 256], replicated, may hold values from 0 to 65535
Outputs:
- loss: float32 [2, 256], replicated
Inputs may be any that keep to these rules, and one draw needn't show every extreme that they name: `routes`: each token names 8 different experts. Among the 16 tokens of one index of expert in one micro-batch and layer, no expert is named by more than 8 tokens, a bound that some block reaches.
All inputs are finite; a program needn't handle non-finite values.
Results may differ from a plain program's by a relative error of at most 0.013.
Values may be sent and summed in bfloat16 or wider, within the bound.
A program may use at most 128 MiB of HBM per device.

v0:
```python
import jax
import jax.numpy as jnp
from jax import lax
from jax.sharding import PartitionSpec as P

routed_scale = 2.5
norm_eps = 1e-06


def shifted(value, axis, steps):
    count = lax.axis_size(axis)
    leading, last = (max(0, -steps), min(count, count - steps))
    return lax.ppermute(value, axis, [(source, source + steps) for source in range(leading, last)])


def from_root(array, axis, root):
    mine = lax.axis_index(axis) == root
    return lax.psum(jnp.where(mine, array, jnp.zeros_like(array)), axis)


def merged(part, axis, combine):
    gathered = jax.tree.map(lambda a: lax.all_gather(a, axis), part)

    def take(source):
        return jax.tree.map(lambda a: lax.dynamic_index_in_dim(a, source, 0, False), gathered)

    return lax.fori_loop(
        1, lax.axis_size(axis), lambda source, state: combine(state, take(source)), take(0)
    )


def slot_tables(route, experts, capacity):
    flat_routes = route.reshape(-1)
    count = flat_routes.shape[0]
    fanout = route.shape[1]
    one_hot = (flat_routes[:, None] == jnp.arange(experts, dtype=jnp.int32)[None, :]).astype(
        jnp.int32
    )
    before = jnp.cumsum(one_hot, axis=0) - one_hot
    place = jnp.sum(before * one_hot, axis=1)
    backward = flat_routes * capacity + place
    match = backward[None, :] == jnp.arange(experts * capacity, dtype=jnp.int32)[:, None]
    valid = jnp.any(match, axis=1)
    source = jnp.sum(
        jnp.where(match, jnp.arange(count, dtype=jnp.int32)[None, :] // fanout, 0), axis=1
    )
    return (source, valid, backward)


def scaled_norm(value, gain):
    widened = value.astype(jnp.float32)
    inverse = lax.rsqrt(jnp.mean(widened * widened, axis=-1, keepdims=True) + norm_eps)
    return (widened * inverse * gain).astype(jnp.bfloat16)


def local(
    stream,
    layer_gain,
    router_weight,
    gate_weight,
    up_weight,
    down_weight,
    routes,
    final_gain,
    head_weight,
    targets,
):
    section = lax.axis_index("pipe")
    sections = lax.axis_size("pipe")
    experts = lax.axis_size("expert")
    micro_count = stream.shape[0]
    rows_here = stream.shape[1]
    fanout = routes.shape[3]
    capacity = max(
        4 * rows_here * fanout // (3 * experts) // 8 * 8,
        (rows_here * fanout + experts - 1) // experts,
    )
    entering = lax.all_gather(stream, "pipe", axis=2, tiled=True)
    width = entering.shape[2]
    gain = layer_gain[0]
    router = router_weight[0]
    w_gate = gate_weight[0, 0]
    w_up = up_weight[0, 0]
    w_down = down_weight[0, 0]
    my_routes = routes[0]

    def expert_work(rows):
        shape_in = rows.shape
        flat_rows = rows.reshape(-1, width)
        gated = jnp.dot(flat_rows, w_gate, preferred_element_type=jnp.float32)
        lifted = jnp.dot(flat_rows, w_up, preferred_element_type=jnp.float32)
        hidden = (jax.nn.silu(gated) * lifted).astype(jnp.bfloat16)
        produced = jnp.dot(hidden, w_down, preferred_element_type=jnp.float32).astype(jnp.bfloat16)
        return produced.reshape(shape_in)

    def apply_layer(value, route):
        normed = scaled_norm(value, gain)
        affinity = jax.nn.sigmoid(jnp.dot(normed, router, preferred_element_type=jnp.float32))
        picked = route[:, :, None] == jnp.arange(experts, dtype=jnp.int32)[None, None, :]
        chosen = jnp.sum(jnp.where(picked, affinity[:, None, :], 0.0), axis=-1)
        weights = routed_scale * chosen / jnp.sum(chosen, axis=-1, keepdims=True)
        source, valid, backward = slot_tables(route, experts, capacity)
        packed = jnp.take(normed, source, axis=0)
        packed = jnp.where(valid[:, None], packed, jnp.zeros_like(packed)).reshape(
            experts, capacity, width
        )
        produced = expert_work(
            lax.all_to_all(packed, "expert", split_axis=0, concat_axis=0, tiled=True)
        )
        returned = lax.all_to_all(produced, "expert", split_axis=0, concat_axis=0, tiled=True)
        collected = jnp.take(returned.reshape(experts * capacity, width), backward, axis=0)
        collected = collected.reshape(rows_here, fanout, width).astype(jnp.float32)
        mixed = jnp.einsum("tk,tkd->td", weights, collected)
        return (value.astype(jnp.float32) + mixed).astype(jnp.bfloat16)

    def tick(tick_now, carry):
        received, finished = carry
        offset_now = tick_now - section
        active = jnp.logical_and(offset_now >= 0, offset_now < micro_count)
        position = jnp.clip(offset_now, 0, micro_count - 1)
        first_input = lax.dynamic_index_in_dim(entering, position, 0, keepdims=False)
        value = jnp.where(section == 0, first_input, received)
        route = lax.dynamic_index_in_dim(my_routes, position, 0, keepdims=False)
        computed = apply_layer(value, route)
        result = jnp.where(active, computed, value)
        store = jnp.logical_and(active, section == sections - 1)
        updated = lax.dynamic_update_index_in_dim(finished, result, position, 0)
        finished = jnp.where(store, updated, finished)
        received = shifted(result, "pipe", 1)
        return (received, finished)

    start_state = jnp.zeros((rows_here, width), jnp.bfloat16)
    start_done = jnp.zeros((micro_count, rows_here, width), jnp.bfloat16)
    received, finished = lax.fori_loop(
        0, micro_count + sections - 1, tick, (start_state, start_done)
    )
    drafted = scaled_norm(finished, final_gain)
    collected_all = lax.all_gather(drafted, "expert", axis=1, tiled=True)
    whole = from_root(collected_all, "pipe", sections - 1)
    flat_states = whole.reshape(-1, width)
    logits = lax.dot_general(
        flat_states, head_weight, (((1,), (1,)), ((), ())), preferred_element_type=jnp.float32
    )
    vocab_rows = head_weight.shape[0]
    offset = lax.axis_index(("pipe", "expert")) * vocab_rows
    wanted = targets.reshape(-1)
    highest = jnp.max(logits, axis=1)
    total = jnp.sum(jnp.exp(logits - highest[:, None]), axis=1)
    columns = jnp.arange(vocab_rows, dtype=jnp.int32)[None, :] + offset
    hit = jnp.sum(jnp.where(columns == wanted[:, None], logits, 0.0), axis=1)

    def combine_stats(earlier, later):
        high_a, total_a, hit_a = earlier
        high_b, total_b, hit_b = later
        larger = jnp.maximum(high_a, high_b)
        joined = total_a * jnp.exp(high_a - larger) + total_b * jnp.exp(high_b - larger)
        return (larger, joined, hit_a + hit_b)

    highest, total, hit = merged((highest, total, hit), ("pipe", "expert"), combine_stats)
    loss = highest + jnp.log(total) - hit
    return loss.reshape(targets.shape)


def solution(mesh):
    in_specs = (
        P(None, "expert", "pipe"),
        P("pipe", None),
        P("pipe", None, None),
        P("pipe", "expert", None, None),
        P("pipe", "expert", None, None),
        P("pipe", "expert", None, None),
        P("pipe", None, "expert", None),
        P(),
        P(("pipe", "expert"), None),
        P(),
    )
    out_specs = P()
    return jax.shard_map(local, mesh=mesh, in_specs=in_specs, out_specs=out_specs, check_vma=False)
```

profile of v0, /device:TPU:1, one launch (start us, length us, event | category | flops | bytes accessed | tf_op | source)
XLA Modules:
  0.0 1412.8 jit_solution(15374143305981384633)
XLA Ops:
  7.5 40.5 %all_gather.24 = bf16[2,16,3584]{1,0,2:T(2,128)(2,1)S(1)} all-gather(bf16[2,16,448]{1,0,2:T(2,128)(2,1)S(1)} %copy.49), channel_id=1, replica_groups=mesh['pipe'=8,'expert'=16] {'pipe'}, dimensions={2}, use_global_device_ids=true | all-gather | bytes 258048 | tf_op jit(solution)/shard_map/all_gather | solution.py:78
  50.1 591.5 %while.36 = (s32[]{:T(128)}, bf16[16,3584]{1,0:T(8,128)(2,1)S(1)}, bf16[2,16,3584]{2,1,0:T(8,128)(2,1)S(1)}, s32[]{:T(128)}, pred[]{:T(512)}, /*index=5*/bf16[2,...) while((s32[]{:T(128)}, bf16[16,3584]{1,0:T(8,128)(2,1)S(1)}, ...), condition=%wide.region_8.9_spmd, body=%wide.region_0.8_spmd.sunk | while | flops 2825062912 | bytes 40041176 | solution.py:134
  53.9 10.4 all-to-all-start
  64.8 15.2 %all-to-all-done = bf16[16,8,3584]{2,1,0:T(8,128)(2,1)S(1)} async-done(((bf16[16,8,3584]{2,1,0:T(8,128)(2,1)}), bf16[16,8,3584]{2,1,0:T(8,128)(2,1)S(1)}, u32[]{:S(2)}, u32[]{:S(2)}) %all-to-all-start) | async-done | bytes 917536 | tf_op jit(solution)/shard_map/while/body/eval_jaxpr/all_to_all | solution.py:108
  84.2 8.3 fusion.81
  97.5 15.2 %all-to-all-done.1 = bf16[16,8,3584]{2,1,0:T(8,128)(2,1)S(1)} async-done(((bf16[16,8,3584]{2,1,0:T(8,128)(2,1)}), bf16[16,8,3584]{2,1,0:T(8,128)(2,1)S(1)}, u32[]{:S(2)}, u32[]{:S(2)}) %all-to-all-start.1) | async-done | bytes 917536 | tf_op jit(solution)/shard_map/while/body/eval_jaxpr/all_to_all | solution.py:110
  126.9 15.2 %all-to-all-done = bf16[16,8,3584]{2,1,0:T(8,128)(2,1)S(1)} async-done(((bf16[16,8,3584]{2,1,0:T(8,128)(2,1)}), bf16[16,8,3584]{2,1,0:T(8,128)(2,1)S(1)}, u32[]{:S(2)}, u32[]{:S(2)}) %all-to-all-start) | async-done | bytes 917536 | tf_op jit(solution)/shard_map/while/body/eval_jaxpr/all_to_all | solution.py:108
  146.3 8.3 fusion.81
  159.5 15.2 %all-to-all-done.1 = bf16[16,8,3584]{2,1,0:T(8,128)(2,1)S(1)} async-done(((bf16[16,8,3584]{2,1,0:T(8,128)(2,1)}), bf16[16,8,3584]{2,1,0:T(8,128)(2,1)S(1)}, u32[]{:S(2)}, u32[]{:S(2)}) %all-to-all-start.1) | async-done | bytes 917536 | tf_op jit(solution)/shard_map/while/body/eval_jaxpr/all_to_all | solution.py:110
  192.2 15.2 %all-to-all-done = bf16[16,8,3584]{2,1,0:T(8,128)(2,1)S(1)} async-done(((bf16[16,8,3584]{2,1,0:T(8,128)(2,1)}), bf16[16,8,3584]{2,1,0:T(8,128)(2,1)S(1)}, u32[]{:S(2)}, u32[]{:S(2)}) %all-to-all-start) | async-done | bytes 917536 | tf_op jit(solution)/shard_map/while/body/eval_jaxpr/all_to_all | solution.py:108
  211.7 8.3 fusion.81
  224.9 15.2 %all-to-all-done.1 = bf16[16,8,3584]{2,1,0:T(8,128)(2,1)S(1)} async-done(((bf16[16,8,3584]{2,1,0:T(8,128)(2,1)}), bf16[16,8,3584]{2,1,0:T(8,128)(2,1)S(1)}, u32[]{:S(2)}, u32[]{:S(2)}) %all-to-all-start.1) | async-done | bytes 917536 | tf_op jit(solution)/shard_map/while/body/eval_jaxpr/all_to_all | solution.py:110
  257.2 15.2 %all-to-all-done = bf16[16,8,3584]{2,1,0:T(8,128)(2,1)S(1)} async-done(((bf16[16,8,3584]{2,1,0:T(8,128)(2,1)}), bf16[16,8,3584]{2,1,0:T(8,128)(2,1)S(1)}, u32[]{:S(2)}, u32[]{:S(2)}) %all-to-all-start) | async-done | bytes 917536 | tf_op jit(solution)/shard_map/while/body/eval_jaxpr/all_to_all | solution.py:108
  276.6 8.3 fusion.81
  289.9 15.2 %all-to-all-done.1 = bf16[16,8,3584]{2,1,0:T(8,128)(2,1)S(1)} async-done(((bf16[16,8,3584]{2,1,0:T(8,128)(2,1)}), bf16[16,8,3584]{2,1,0:T(8,128)(2,1)S(1)}, u32[]{:S(2)}, u32[]{:S(2)}) %all-to-all-start.1) | async-done | bytes 917536 | tf_op jit(solution)/shard_map/while/body/eval_jaxpr/all_to_all | solution.py:110
  322.3 15.2 %all-to-all-done = bf16[16,8,3584]{2,1,0:T(8,128)(2,1)S(1)} async-done(((bf16[16,8,3584]{2,1,0:T(8,128)(2,1)}), bf16[16,8,3584]{2,1,0:T(8,128)(2,1)S(1)}, u32[]{:S(2)}, u32[]{:S(2)}) %all-to-all-start) | async-done | bytes 917536 | tf_op jit(solution)/shard_map/while/body/eval_jaxpr/all_to_all | solution.py:108
  354.9 15.2 %all-to-all-done.1 = bf16[16,8,3584]{2,1,0:T(8,128)(2,1)S(1)} async-done(((bf16[16,8,3584]{2,1,0:T(8,128)(2,1)}), bf16[16,8,3584]{2,1,0:T(8,128)(2,1)S(1)}, u32[]{:S(2)}, u32[]{:S(2)}) %all-to-all-start.1) | async-done | bytes 917536 | tf_op jit(solution)/shard_map/while/body/eval_jaxpr/all_to_all | solution.py:110
  388.2 15.2 %all-to-all-done = bf16[16,8,3584]{2,1,0:T(8,128)(2,1)S(1)} async-done(((bf16[16,8,3584]{2,1,0:T(8,128)(2,1)}), bf16[16,8,3584]{2,1,0:T(8,128)(2,1)S(1)}, u32[]{:S(2)}, u32[]{:S(2)}) %all-to-all-start) | async-done | bytes 917536 | tf_op jit(solution)/shard_map/while/body/eval_jaxpr/all_to_all | solution.py:108
  407.6 8.3 fusion.81
  420.8 15.2 %all-to-all-done.1 = bf16[16,8,3584]{2,1,0:T(8,128)(2,1)S(1)} async-done(((bf16[16,8,3584]{2,1,0:T(8,128)(2,1)}), bf16[16,8,3584]{2,1,0:T(8,128)(2,1)S(1)}, u32[]{:S(2)}, u32[]{:S(2)}) %all-to-all-start.1) | async-done | bytes 917536 | tf_op jit(solution)/shard_map/while/body/eval_jaxpr/all_to_all | solution.py:110
  454.1 15.2 %all-to-all-done = bf16[16,8,3584]{2,1,0:T(8,128)(2,1)S(1)} async-done(((bf16[16,8,3584]{2,1,0:T(8,128)(2,1)}), bf16[16,8,3584]{2,1,0:T(8,128)(2,1)S(1)}, u32[]{:S(2)}, u32[]{:S(2)}) %all-to-all-start) | async-done | bytes 917536 | tf_op jit(solution)/shard_map/while/body/eval_jaxpr/all_to_all | solution.py:108
  486.7 15.2 %all-to-all-done.1 = bf16[16,8,3584]{2,1,0:T(8,128)(2,1)S(1)} async-done(((bf16[16,8,3584]{2,1,0:T(8,128)(2,1)}), bf16[16,8,3584]{2,1,0:T(8,128)(2,1)S(1)}, u32[]{:S(2)}, u32[]{:S(2)}) %all-to-all-start.1) | async-done | bytes 917536 | tf_op jit(solution)/shard_map/while/body/eval_jaxpr/all_to_all | solution.py:110
  519.9 15.2 %all-to-all-done = bf16[16,8,3584]{2,1,0:T(8,128)(2,1)S(1)} async-done(((bf16[16,8,3584]{2,1,0:T(8,128)(2,1)}), bf16[16,8,3584]{2,1,0:T(8,128)(2,1)S(1)}, u32[]{:S(2)}, u32[]{:S(2)}) %all-to-all-start) | async-done | bytes 917536 | tf_op jit(solution)/shard_map/while/body/eval_jaxpr/all_to_all | solution.py:108
  552.6 15.2 %all-to-all-done.1 = bf16[16,8,3584]{2,1,0:T(8,128)(2,1)S(1)} async-done(((bf16[16,8,3584]{2,1,0:T(8,128)(2,1)}), bf16[16,8,3584]{2,1,0:T(8,128)(2,1)S(1)}, u32[]{:S(2)}, u32[]{:S(2)}) %all-to-all-start.1) | async-done | bytes 917536 | tf_op jit(solution)/shard_map/while/body/eval_jaxpr/all_to_all | solution.py:110
  585.8 15.2 %all-to-all-done = bf16[16,8,3584]{2,1,0:T(8,128)(2,1)S(1)} async-done(((bf16[16,8,3584]{2,1,0:T(8,128)(2,1)}), bf16[16,8,3584]{2,1,0:T(8,128)(2,1)S(1)}, u32[]{:S(2)}, u32[]{:S(2)}) %all-to-all-start) | async-done | bytes 917536 | tf_op jit(solution)/shard_map/while/body/eval_jaxpr/all_to_all | solution.py:108
  618.5 15.2 %all-to-all-done.1 = bf16[16,8,3584]{2,1,0:T(8,128)(2,1)S(1)} async-done(((bf16[16,8,3584]{2,1,0:T(8,128)(2,1)}), bf16[16,8,3584]{2,1,0:T(8,128)(2,1)S(1)}, u32[]{:S(2)}, u32[]{:S(2)}) %all-to-all-start.1) | async-done | bytes 917536 | tf_op jit(solution)/shard_map/while/body/eval_jaxpr/all_to_all | solution.py:110
  642.7 57.9 %all-gather.8.cloned.1.call-done = bf16[2,256,3584]{2,1,0:T(8,128)(2,1)} async-done(((bf16[2,16,3584]{2,1,0:T(8,128)(2,1)}), bf16[2,256,3584]{2,1,0:T(8,128)(2,1)}) %all-gather.8.cloned.1.call-update) | async-done | bytes 3670032 | tf_op jit(solution)/shard_map/all_gather | solution.py:138
  703.3 163.0 %all-reduce.2.cloned.1.call-done = bf16[512,3584]{1,0:T(8,128)(2,1)} async-done(((bf16[512,3584]{1,0:T(8,128)(2,1)}), bf16[512,3584]{1,0:T(8,128)(2,1)}) %all-reduce.2.cloned.1.call-update) | async-done | bytes 3670032 | tf_op jit(solution)/shard_map/psum | solution.py:18
  871.8 176.5 %all-gather.4 = f32[128,1,512]{2,1,0:T(1,128)S(1)} all-gather(f32[1,1,512]{2,1,0:T(1,128)S(1)} %bitcast.144), channel_id=3, replica_groups=mesh['pipe'=8,'expert'=16] {'pipe','expert'}, dimensions={0}, use_global_device_ids=true | all-gather | bytes 264192 | tf_op jit(solution)/shard_map/all_gather | solution.py:22
  1048.3 171.2 %all-gather.5 = f32[128,1,512]{2,1,0:T(1,128)S(1)} all-gather(f32[1,1,512]{2,1,0:T(1,128)S(1)} %bitcast.143), channel_id=4, replica_groups=mesh['pipe'=8,'expert'=16] {'pipe','expert'}, dimensions={0}, use_global_device_ids=true | all-gather | bytes 264192 | tf_op jit(solution)/shard_map/all_gather | solution.py:22
  1219.5 174.0 %all-gather.3 = f32[128,1,512]{2,1,0:T(1,128)S(1)} all-gather(f32[1,1,512]{2,1,0:T(1,128)S(1)} %bitcast.142), channel_id=2, replica_groups=mesh['pipe'=8,'expert'=16] {'pipe','expert'}, dimensions={0}, use_global_device_ids=true | all-gather | bytes 264192 | tf_op jit(solution)/shard_map/all_gather | solution.py:22
  1393.5 11.8 while.37
  (923 shorter events, 284.4 us)
Async XLA Ops:
  6.5 43.5 %copy-start = (bf16[1,3584,16]{1,2,0:T(8,128)(2,1)S(1)}, bf16[1,3584,16]{1,2,0:T(8,128)(2,1)}, u32[]{:S(2)}) copy-start(bf16[1,3584,16]{1,2,0:T(8,128)(2,1)} %param.16) | copy-start | bytes 344068
  6.5 43.5 %copy-start.1 = (f32[1,3584]{1,0:T(1,128)S(1)}, f32[1,3584]{1,0:T(1,128)}, u32[]{:S(2)}) copy-start(f32[1,3584]{1,0:T(1,128)} %param.15) | copy-start | bytes 43012
  6.5 694.0 %all-gather.8.cloned.1.call-start = ((), (), s32[]{:S(2)}) async-start(), calls=%async_computation.2 | async-start | bytes 3899392 | tf_op jit(solution)/shard_map/all_gather | solution.py:138
  50.1 591.7 %copy-start.3 = (f32[3584]{0:T(1024)S(1)}, f32[3584]{0:T(1024)}, u32[]{:S(2)}) copy-start(f32[3584]{0:T(1024)} %param.21) | copy-start | bytes 43012
  53.9 26.1 %all-to-all-start = ((bf16[16,8,3584]{2,1,0:T(8,128)(2,1)}), bf16[16,8,3584]{2,1,0:T(8,128)(2,1)S(1)}, u32[]{:S(2)}, u32[]{:S(2)}) async-start(bf16[16,8,3584]{2,1,0:T(8,128)(2,1)} %fusion.79), calls=%async_computation | async-start | bytes 1835008 | tf_op jit(solution)/shard_map/while/body/eval_jaxpr/all_to_all | solution.py:108
  92.5 20.2 %all-to-all-start.1 = ((bf16[16,8,3584]{2,1,0:T(8,128)(2,1)}), bf16[16,8,3584]{2,1,0:T(8,128)(2,1)S(1)}, u32[]{:S(2)}, u32[]{:S(2)}) async-start(bf16[16,8,3584]{2,1,0:T(8,128)(2,1)} %fusion.81), calls=%async_computation.1 | async-start | bytes 1835008 | tf_op jit(solution)/shard_map/while/body/eval_jaxpr/all_to_all | solution.py:110
  114.3 3.1 collective-permute-start
  121.2 20.8 %all-to-all-start = ((bf16[16,8,3584]{2,1,0:T(8,128)(2,1)}), bf16[16,8,3584]{2,1,0:T(8,128)(2,1)S(1)}, u32[]{:S(2)}, u32[]{:S(2)}) async-start(bf16[16,8,3584]{2,1,0:T(8,128)(2,1)} %fusion.79), calls=%async_computation | async-start | bytes 1835008 | tf_op jit(solution)/shard_map/while/body/eval_jaxpr/all_to_all | solution.py:108
  154.5 20.2 %all-to-all-start.1 = ((bf16[16,8,3584]{2,1,0:T(8,128)(2,1)}), bf16[16,8,3584]{2,1,0:T(8,128)(2,1)S(1)}, u32[]{:S(2)}, u32[]{:S(2)}) async-start(bf16[16,8,3584]{2,1,0:T(8,128)(2,1)} %fusion.81), calls=%async_computation.1 | async-start | bytes 1835008 | tf_op jit(solution)/shard_map/while/body/eval_jaxpr/all_to_all | solution.py:110
  176.4 5.8 collective-permute-start
  186.0 21.4 %all-to-all-start = ((bf16[16,8,3584]{2,1,0:T(8,128)(2,1)}), bf16[16,8,3584]{2,1,0:T(8,128)(2,1)S(1)}, u32[]{:S(2)}, u32[]{:S(2)}) async-start(bf16[16,8,3584]{2,1,0:T(8,128)(2,1)} %fusion.79), calls=%async_computation | async-start | bytes 1835008 | tf_op jit(solution)/shard_map/while/body/eval_jaxpr/all_to_all | solution.py:108
  219.9 20.2 %all-to-all-start.1 = ((bf16[16,8,3584]{2,1,0:T(8,128)(2,1)}), bf16[16,8,3584]{2,1,0:T(8,128)(2,1)S(1)}, u32[]{:S(2)}, u32[]{:S(2)}) async-start(bf16[16,8,3584]{2,1,0:T(8,128)(2,1)} %fusion.81), calls=%async_computation.1 | async-start | bytes 1835008 | tf_op jit(solution)/shard_map/while/body/eval_jaxpr/all_to_all | solution.py:110
  241.8 5.4 collective-permute-start
  251.0 21.4 %all-to-all-start = ((bf16[16,8,3584]{2,1,0:T(8,128)(2,1)}), bf16[16,8,3584]{2,1,0:T(8,128)(2,1)S(1)}, u32[]{:S(2)}, u32[]{:S(2)}) async-start(bf16[16,8,3584]{2,1,0:T(8,128)(2,1)} %fusion.79), calls=%async_computation | async-start | bytes 1835008 | tf_op jit(solution)/shard_map/while/body/eval_jaxpr/all_to_all | solution.py:108
  284.9 20.2 %all-to-all-start.1 = ((bf16[16,8,3584]{2,1,0:T(8,128)(2,1)}), bf16[16,8,3584]{2,1,0:T(8,128)(2,1)S(1)}, u32[]{:S(2)}, u32[]{:S(2)}) async-start(bf16[16,8,3584]{2,1,0:T(8,128)(2,1)} %fusion.81), calls=%async_computation.1 | async-start | bytes 1835008 | tf_op jit(solution)/shard_map/while/body/eval_jaxpr/all_to_all | solution.py:110
  306.7 5.5 collective-permute-start
  316.1 21.4 %all-to-all-start = ((bf16[16,8,3584]{2,1,0:T(8,128)(2,1)}), bf16[16,8,3584]{2,1,0:T(8,128)(2,1)S(1)}, u32[]{:S(2)}, u32[]{:S(2)}) async-start(bf16[16,8,3584]{2,1,0:T(8,128)(2,1)} %fusion.79), calls=%async_computation | async-start | bytes 1835008 | tf_op jit(solution)/shard_map/while/body/eval_jaxpr/all_to_all | solution.py:108
  350.0 20.2 %all-to-all-start.1 = ((bf16[16,8,3584]{2,1,0:T(8,128)(2,1)}), bf16[16,8,3584]{2,1,0:T(8,128)(2,1)S(1)}, u32[]{:S(2)}, u32[]{:S(2)}) async-start(bf16[16,8,3584]{2,1,0:T(8,128)(2,1)} %fusion.81), calls=%async_computation.1 | async-start | bytes 1835008 | tf_op jit(solution)/shard_map/while/body/eval_jaxpr/all_to_all | solution.py:110
  371.8 6.3 collective-permute-start
  381.9 21.4 %all-to-all-start = ((bf16[16,8,3584]{2,1,0:T(8,128)(2,1)}), bf16[16,8,3584]{2,1,0:T(8,128)(2,1)S(1)}, u32[]{:S(2)}, u32[]{:S(2)}) async-start(bf16[16,8,3584]{2,1,0:T(8,128)(2,1)} %fusion.79), calls=%async_computation | async-start | bytes 1835008 | tf_op jit(solution)/shard_map/while/body/eval_jaxpr/all_to_all | solution.py:108
  415.8 20.2 %all-to-all-start.1 = ((bf16[16,8,3584]{2,1,0:T(8,128)(2,1)}), bf16[16,8,3584]{2,1,0:T(8,128)(2,1)S(1)}, u32[]{:S(2)}, u32[]{:S(2)}) async-start(bf16[16,8,3584]{2,1,0:T(8,128)(2,1)} %fusion.81), calls=%async_computation.1 | async-start | bytes 1835008 | tf_op jit(solution)/shard_map/while/body/eval_jaxpr/all_to_all | solution.py:110
  437.7 6.3 collective-permute-start
  447.8 21.4 %all-to-all-start = ((bf16[16,8,3584]{2,1,0:T(8,128)(2,1)}), bf16[16,8,3584]{2,1,0:T(8,128)(2,1)S(1)}, u32[]{:S(2)}, u32[]{:S(2)}) async-start(bf16[16,8,3584]{2,1,0:T(8,128)(2,1)} %fusion.79), calls=%async_computation | async-start | bytes 1835008 | tf_op jit(solution)/shard_map/while/body/eval_jaxpr/all_to_all | solution.py:108
  481.7 20.2 %all-to-all-start.1 = ((bf16[16,8,3584]{2,1,0:T(8,128)(2,1)}), bf16[16,8,3584]{2,1,0:T(8,128)(2,1)S(1)}, u32[]{:S(2)}, u32[]{:S(2)}) async-start(bf16[16,8,3584]{2,1,0:T(8,128)(2,1)} %fusion.81), calls=%async_computation.1 | async-start | bytes 1835008 | tf_op jit(solution)/shard_map/while/body/eval_jaxpr/all_to_all | solution.py:110
  503.6 6.3 collective-permute-start
  513.7 21.4 %all-to-all-start = ((bf16[16,8,3584]{2,1,0:T(8,128)(2,1)}), bf16[16,8,3584]{2,1,0:T(8,128)(2,1)S(1)}, u32[]{:S(2)}, u32[]{:S(2)}) async-start(bf16[16,8,3584]{2,1,0:T(8,128)(2,1)} %fusion.79), calls=%async_computation | async-start | bytes 1835008 | tf_op jit(solution)/shard_map/while/body/eval_jaxpr/all_to_all | solution.py:108
  547.6 20.2 %all-to-all-start.1 = ((bf16[16,8,3584]{2,1,0:T(8,128)(2,1)}), bf16[16,8,3584]{2,1,0:T(8,128)(2,1)S(1)}, u32[]{:S(2)}, u32[]{:S(2)}) async-start(bf16[16,8,3584]{2,1,0:T(8,128)(2,1)} %fusion.81), calls=%async_computation.1 | async-start | bytes 1835008 | tf_op jit(solution)/shard_map/while/body/eval_jaxpr/all_to_all | solution.py:110
  569.5 6.3 collective-permute-start
  579.6 21.4 %all-to-all-start = ((bf16[16,8,3584]{2,1,0:T(8,128)(2,1)}), bf16[16,8,3584]{2,1,0:T(8,128)(2,1)S(1)}, u32[]{:S(2)}, u32[]{:S(2)}) async-start(bf16[16,8,3584]{2,1,0:T(8,128)(2,1)} %fusion.79), calls=%async_computation | async-start | bytes 1835008 | tf_op jit(solution)/shard_map/while/body/eval_jaxpr/all_to_all | solution.py:108
  613.5 20.2 %all-to-all-start.1 = ((bf16[16,8,3584]{2,1,0:T(8,128)(2,1)}), bf16[16,8,3584]{2,1,0:T(8,128)(2,1)S(1)}, u32[]{:S(2)}, u32[]{:S(2)}) async-start(bf16[16,8,3584]{2,1,0:T(8,128)(2,1)} %fusion.81), calls=%async_computation.1 | async-start | bytes 1835008 | tf_op jit(solution)/shard_map/while/body/eval_jaxpr/all_to_all | solution.py:110
  635.3 6.3 collective-permute-start
  642.6 223.6 %all-reduce.2.cloned.1.call-start = ((), (), s32[]{:S(2)}) async-start(), calls=%async_computation.3 | async-start | bytes 7340032 | tf_op jit(solution)/shard_map/psum | solution.py:18
  (2 other events, 44.2 us)
Sparse Core Ops, SparseCore 0:
  642.7 57.7 all-gather.7
  703.1 163.1 all-reduce.1
where the time goes:
time: 1420 us; the launch traced here: 1410 us
  blocking collectives  562 us (40%)
  waiting for transfers between devices  511 us (36%)
  starting transfers between devices  131 us (9%)
  matrix products  123 us (9%)
  local copies, waits for them, and re-layouts  36.2 us (3%)
  other arithmetic  30.6 us (2%)
    all_gather x3, blocking collectives, merged(): gathered = jax.tree.map(lambda a: lax.all_gather(a, axis), part)  522 us
    psum x1, waiting for transfers between devices, from_root(): return lax.psum(jnp.where(mine, array, jnp.zeros_like(array)), axis)  163 us
    all_to_all x9, waiting for transfers between devices, apply_layer(): lax.all_to_all(produced, 'expert', split_axis=0, concat_axis=0, tiled=True)  137 us
    all_to_all x9, waiting for transfers between devices, apply_layer(): lax.all_to_all(packed, 'expert', split_axis=0, concat_axis=0, tiled=True)  137 us
    dot_general x9, matrix products, expert_work(): jnp.dot(hidden, w_down, preferred_element_type=jnp.float32)  74.4 us
    all_gather x1, waiting for transfers between devices, local(): collected_all = lax.all_gather(drafted, 'expert', axis=1, tiled=True)  57.9 us
    all_to_all x9, starting transfers between devices, apply_layer(): lax.all_to_all(packed, 'expert', split_axis=0, concat_axis=0, tiled=True)  55.7 us
    all_gather x1, blocking collectives, local(): entering = lax.all_gather(stream, 'pipe', axis=2, tiled=True)  40.5 us
  transfers between devices with their start and end apart: 29, of which 29 were waited for; matrix products, arithmetic and copies ran while one was open for 1% of the time, Pallas kernels for 0%

commit v1 on v0

v1 whole, which is shorter than its diff:
```python
import functools

import jax
import jax.numpy as jnp
from jax import lax
from jax.experimental import pallas as pl
from jax.experimental.pallas import tpu as pltpu
from jax.sharding import PartitionSpec as P

routed_scale = 2.5
norm_eps = 1e-06
MESH = pl.DeviceIdType.MESH
f32 = jnp.float32
bf16 = jnp.bfloat16


def iota(shape, axis):
    return lax.broadcasted_iota(jnp.int32, shape, axis)


def dot(a, b):
    return jnp.dot(a, b, preferred_element_type=f32)


def dot_nt(a, b):
    return lax.dot_general(a, b, (((1,), (1,)), ((), ())), preferred_element_type=f32)


def kernel(
    sections,
    experts,
    stream,
    gain,
    router,
    w_gate,
    w_up,
    w_down,
    routes,
    final_gain,
    head,
    targets,
    loss,
    vg,
    vu,
    vd,
    vh,
    gath,
    xin,
    packed,
    recv,
    prod,
    ret,
    hidden,
    rows_in,
    hop,
    fin,
    dall,
    logits,
    spread,
    fold,
    stat,
    stat_pipe,
    stat_mid,
    stat_all,
    w_sem,
    head_sem,
    head_send,
    head_recv,
    stream_send,
    stream_recv,
    disp_send,
    disp_recv,
    back_send,
    back_recv,
    hop_send,
    hop_recv,
    fin_send,
    fin_recv,
    dall_send,
    dall_recv,
    stat_send,
    stat_recv,
):
    micros, tok, part = stream.shape
    half = xin.shape[2]
    width = 2 * half
    cap = 8
    pairs = experts // 2
    slots = experts * cap
    vdev = head.shape[0]
    p = lax.axis_index("pipe")
    e = lax.axis_index("expert")
    chip = e // 2
    core = lax.rem(e, 2)
    last = sections - 1

    def local(src, dst, sem):
        return pltpu.make_async_copy(src, dst, sem)

    def to(src, dst, send, recv_, device):
        return pltpu.make_async_remote_copy(
            src_ref=src, dst_ref=dst, send_sem=send, recv_sem=recv_, device_id=device, device_id_type=MESH
        )

    def drain(ref, sem):
        pltpu.make_async_copy(ref, ref, sem).wait()

    def other_expert(k):
        return lax.rem(e + k, experts)

    def other_section(k):
        return lax.rem(p + k, sections)

    def other_chip(k):
        return 2 * lax.rem(chip + k, pairs) + core

    def each(count, body):
        def step(k, carry):
            body(k)
            return carry

        lax.fori_loop(1, count, step, 0)

    weights = [
        local(w_gate, vg, w_sem.at[0]),
        local(w_up, vu, w_sem.at[1]),
        local(w_down, vd, w_sem.at[2]),
    ]
    for copy in weights:
        copy.start()
    own_head = local(head, vh.at[core], head_sem)
    own_head.start()

    barrier = pltpu.get_barrier_semaphore()

    def greet(device):
        pl.semaphore_signal(barrier, inc=1, device_id=device, device_id_type=MESH)

    each(experts, lambda k: greet((p, other_expert(k))))
    each(sections, lambda k: greet((other_section(k), e)))
    pl.semaphore_wait(barrier, experts + sections - 2)

    stream_out = to(stream, gath.at[p], stream_send, stream_recv, (0, e))

    @pl.when(p > 0)
    def _():
        stream_out.start()

    @pl.when(p == 0)
    def _():
        local(stream, gath.at[0], stream_recv).start()

    head_out = to(head, vh.at[core], head_send, head_recv, (p, 2 * chip + 1 - core))
    head_out.start()

    expert_of = (iota((experts, 2 * slots), 1) // (2 * cap) == iota((experts, 2 * slots), 0)).astype(bf16)
    expert_of_t = (iota((2 * slots, experts), 0) // (2 * cap) == iota((2 * slots, experts), 1)).astype(bf16)
    earlier = (iota((tok, tok), 1) < iota((tok, tok), 0)).astype(bf16)

    def tables(m):
        route = routes[m]
        member = jnp.zeros((tok, experts), f32)
        for k in range(route.shape[1]):
            member = member + (route[:, k : k + 1] == iota((tok, experts), 1)).astype(f32)
        place = dot(earlier, member.astype(bf16))
        code = jnp.where(member > 0, place, -1.0).astype(bf16)
        return member, code

    for m in range(micros):
        member, code = tables(m)
        chosen = dot_nt(expert_of_t, code)
        row = iota((2 * slots, tok), 0)
        valid = chosen == lax.rem(row, cap).astype(f32)
        side = lax.rem(row // cap, 2)
        spread[m] = jnp.concatenate(
            [(valid & (side == 0)).astype(bf16), (valid & (side == 1)).astype(bf16)], axis=1
        )

    gather_row = iota((2 * slots, 2 * slots), 0)
    gather_col = iota((2 * slots, 2 * slots), 1)

    def interleaved(index):
        side = index // slots
        source = lax.rem(index, slots) // cap
        return source * 2 * cap + side * cap + lax.rem(index, cap)

    apart = (interleaved(gather_row) == gather_col).astype(bf16)
    together = (interleaved(gather_col) == gather_row).astype(bf16)

    @pl.when(p == 0)
    def _():
        drain(gath, stream_recv)
        per = sections // 2
        for m in range(micros):
            for side in range(2):
                for j in range(per):
                    xin[m, side * tok : (side + 1) * tok, j * part : (j + 1) * part] = gath[side * per + j, m]

    def normed_of(value, gain_ref):
        wide = value.astype(f32)
        square = jnp.sum(wide * wide, axis=1, keepdims=True)
        mean = (square[:tok] + square[tok:]) / width
        inverse = lax.rsqrt(mean + norm_eps)
        first = wide[:tok] * inverse * gain_ref[:, :half]
        second = wide[tok:] * inverse * gain_ref[:, half:]
        return jnp.concatenate([first, second], axis=0).astype(bf16)

    def dispatch(m):
        @pl.when(p > 0)
        def _():
            drain(xin.at[m], hop_recv.at[m])

        normed = normed_of(xin[m], gain)
        packed[m] = dot(spread[m], normed).astype(bf16)

        def send(k):
            peer = other_expert(k)
            to(
                packed.at[m, pl.ds(pl.multiple_of(peer * 2 * cap, 16), 2 * cap)],
                recv.at[m, pl.ds(pl.multiple_of(e * 2 * cap, 16), 2 * cap)],
                disp_send.at[m],
                disp_recv.at[m],
                (p, peer),
            ).start()

        each(experts, send)
        mine = pl.ds(pl.multiple_of(e * 2 * cap, 16), 2 * cap)
        local(packed.at[m, mine], recv.at[m, mine], disp_recv.at[m]).start()
        member, code = tables(m)
        affinity = jax.nn.sigmoid(dot(normed[:tok], router[:half]) + dot(normed[tok:], router[half:])) * member
        weight = routed_scale * affinity / jnp.sum(affinity, axis=1, keepdims=True)
        upper = weight.astype(bf16)
        lower = (weight - upper.astype(f32)).astype(bf16)
        chosen = dot(code, expert_of)
        column = iota((tok, 2 * slots), 1)
        valid = chosen == lax.rem(column, cap).astype(f32)
        side = lax.rem(column // cap, 2)
        upper = dot(upper, expert_of)
        lower = dot(lower, expert_of)
        one = valid & (side == 0)
        two = valid & (side == 1)
        fold[m] = jnp.concatenate(
            [jnp.where(one, upper, 0.0), jnp.where(two, upper, 0.0), jnp.where(one, lower, 0.0), jnp.where(two, lower, 0.0)],
            axis=0,
        ).astype(bf16)

    def expert_work(m):
        drain(recv.at[m], disp_recv.at[m])
        if m == 0:
            for copy in weights:
                copy.wait()
        rows_in[...] = dot(apart, recv[m]).astype(bf16)
        tile = min(256, hidden.shape[1])

        def up(n, carry):
            cols = pl.ds(pl.multiple_of(n * tile, tile), tile)
            gated = dot(rows_in[:slots], vg[:half, cols]) + dot(rows_in[slots:], vg[half:, cols])
            lifted = dot(rows_in[:slots], vu[:half, cols]) + dot(rows_in[slots:], vu[half:, cols])
            hidden[:, cols] = (gated / (1.0 + jnp.exp(-gated)) * lifted).astype(bf16)
            return carry

        lax.fori_loop(0, hidden.shape[1] // tile, up, 0)

        def down(n, carry):
            first = pl.ds(pl.multiple_of(n * tile, 128), tile)
            second = pl.ds(pl.multiple_of(half + n * tile, 128), tile)
            both = jnp.concatenate([dot(hidden[...], vd[:, first]), dot(hidden[...], vd[:, second])], axis=0)
            prod[m, :, first] = dot(together, both.astype(bf16)).astype(bf16)
            return carry

        lax.fori_loop(0, half // tile, down, 0)

        def send(k):
            peer = other_expert(k)
            to(
                prod.at[m, pl.ds(pl.multiple_of(peer * 2 * cap, 16), 2 * cap)],
                ret.at[m, pl.ds(pl.multiple_of(e * 2 * cap, 16), 2 * cap)],
                back_send.at[m],
                back_recv.at[m],
                (p, peer),
            ).start()

        each(experts, send)
        mine = pl.ds(pl.multiple_of(e * 2 * cap, 16), 2 * cap)
        local(prod.at[m, mine], ret.at[m, mine], back_recv.at[m]).start()

    def combine(m):
        drain(ret.at[m], back_recv.at[m])
        mixed = dot(fold[m], ret[m])
        out = (xin[m].astype(f32) + mixed[: 2 * tok] + mixed[2 * tok :]).astype(bf16)

        @pl.when(p < last)
        def _():
            hop[m] = out
            to(hop.at[m], xin.at[m], hop_send.at[m], hop_recv.at[m], (p + 1, e)).start()

        @pl.when(p == last)
        def _():
            fin[m] = normed_of(out, final_gain)
            each(
                sections,
                lambda k: to(fin.at[m], fin.at[m], fin_send.at[m], fin_recv.at[m], (other_section(k), e)).start(),
            )

    def share(m):
        @pl.when(p < last)
        def _():
            drain(fin.at[m], fin_recv.at[m])

        each(
            pairs,
            lambda k: to(
                fin.at[m], dall.at[m, chip], dall_send.at[m], dall_recv.at[m], (p, other_chip(k))
            ).start(),
        )
        local(fin.at[m], dall.at[m, chip], dall_recv.at[m]).start()

    def head_work(m):
        drain(dall.at[m], dall_recv.at[m])
        if m == 0:
            own_head.wait()
            head_out.wait()
        states = dall[m].reshape(pairs, 2, tok, half)
        first = states[:, 0].reshape(pairs * tok, half)
        second = states[:, 1].reshape(pairs * tok, half)
        tile = min(256, vdev)
        per = vdev // tile

        def step(n, carry):
            block = vh.at[n // per]
            rows = pl.ds(pl.multiple_of(lax.rem(n, per) * tile, tile), tile)
            value = dot_nt(block[rows, :half], first) + dot_nt(block[rows, half:], second)
            logits[pl.ds(pl.multiple_of(n * tile, tile), tile)] = value
            return carry

        lax.fori_loop(0, 2 * per, step, 0)
        value = logits[...]
        highest = jnp.max(value, axis=0, keepdims=True)
        total = jnp.sum(jnp.exp(value - highest), axis=0, keepdims=True)
        entry = iota(value.shape, 0) + (p * experts + 2 * chip) * vdev
        hit = jnp.sum(jnp.where(entry == targets[core, m][None, :], value, 0.0), axis=0, keepdims=True)
        stat[:, m * pairs * tok : (m + 1) * pairs * tok] = jnp.concatenate(
            [highest, total, hit, jnp.zeros((5, pairs * tok), f32)], axis=0
        )

    dispatch(0)
    expert_work(0)
    dispatch(1)
    combine(0)

    @pl.when(p == last)
    def _():
        share(0)

    expert_work(1)
    combine(1)

    @pl.when(p < last)
    def _():
        share(0)

    head_work(0)
    share(1)
    head_work(1)

    def merged(parts):
        highest = functools.reduce(jnp.maximum, [part_[0:1] for part_ in parts])
        total = sum(part_[1:2] * jnp.exp(part_[0:1] - highest) for part_ in parts)
        hit = sum(part_[2:3] for part_ in parts)
        return highest, total, hit

    each(
        sections,
        lambda k: to(stat, stat_pipe.at[p], stat_send.at[0], stat_recv.at[0], (other_section(k), e)).start(),
    )
    local(stat, stat_pipe.at[p], stat_recv.at[0]).start()
    drain(stat_pipe, stat_recv.at[0])
    highest, total, hit = merged([stat_pipe[j] for j in range(sections)])
    stat_mid[...] = jnp.concatenate([highest, total, hit, jnp.zeros((5, highest.shape[1]), f32)], axis=0)
    each(
        experts,
        lambda k: to(stat_mid, stat_all.at[e], stat_send.at[1], stat_recv.at[1], (p, other_expert(k))).start(),
    )
    local(stat_mid, stat_all.at[e], stat_recv.at[1]).start()
    drain(stat_all, stat_recv.at[1])
    for c in range(2):
        highest, total, hit = merged([stat_all[2 * j + c] for j in range(pairs)])
        loss[c : c + 1, :] = highest + jnp.log(total) - hit

    @pl.when(p > 0)
    def _():
        drain(stream, stream_send)

    for m in range(micros):
        for buffer, sem in ((packed, disp_send), (prod, back_send)):
            drain(buffer.at[m, pl.ds(0, 2 * slots - 2 * cap)], sem.at[m])

        @pl.when(p < last)
        def _():
            drain(hop.at[m], hop_send.at[m])

        @pl.when(p == last)
        def _():
            for _ in range(sections - 1):
                drain(fin.at[m], fin_send.at[m])

        drain(dall.at[m, pl.ds(0, pairs - 1)], dall_send.at[m])
    drain(stat_pipe.at[pl.ds(0, sections - 1)], stat_send.at[0])
    drain(stat_all.at[pl.ds(0, experts - 1)], stat_send.at[1])


def local(
    stream,
    layer_gain,
    router_weight,
    gate_weight,
    up_weight,
    down_weight,
    routes,
    final_gain,
    head_weight,
    targets,
):
    sections = lax.axis_size("pipe")
    experts = lax.axis_size("expert")
    micros, tok, part = stream.shape
    width = layer_gain.shape[1]
    half = width // 2
    hidden = gate_weight.shape[3]
    vdev = head_weight.shape[0]
    pairs = experts // 2
    slots = experts * 8
    by_core = targets.reshape(micros, pairs, 2, tok).transpose(2, 0, 1, 3).reshape(2, micros, pairs * tok)
    dma = pltpu.SemaphoreType.DMA
    vmem = pl.BlockSpec(memory_space=pltpu.VMEM)
    hbm = pl.BlockSpec(memory_space=pl.ANY)
    loss = pl.pallas_call(
        functools.partial(kernel, sections, experts),
        out_shape=jax.ShapeDtypeStruct((2, micros * pairs * tok), f32),
        in_specs=[hbm, vmem, vmem, hbm, hbm, hbm, vmem, vmem, hbm, vmem],
        out_specs=vmem,
        scratch_shapes=[
            pltpu.VMEM((width, hidden), bf16),
            pltpu.VMEM((width, hidden), bf16),
            pltpu.VMEM((hidden, width), bf16),
            pltpu.VMEM((2, vdev, width), bf16),
            pltpu.VMEM((sections, micros, tok, part), bf16),
            pltpu.VMEM((micros, 2 * tok, half), bf16),
            pltpu.VMEM((micros, 2 * slots, half), bf16),
            pltpu.VMEM((micros, 2 * slots, half), bf16),
            pltpu.VMEM((micros, 2 * slots, half), bf16),
            pltpu.VMEM((micros, 2 * slots, half), bf16),
            pltpu.VMEM((slots, hidden), bf16),
            pltpu.VMEM((2 * slots, half), bf16),
            pltpu.VMEM((micros, 2 * tok, half), bf16),
            pltpu.VMEM((micros, 2 * tok, half), bf16),
            pltpu.VMEM((micros, pairs, 2 * tok, half), bf16),
            pltpu.VMEM((2 * vdev, pairs * tok), f32),
            pltpu.VMEM((micros, 2 * slots, 2 * tok), bf16),
            pltpu.VMEM((micros, 4 * tok, 2 * slots), bf16),
            pltpu.VMEM((8, micros * pairs * tok), f32),
            pltpu.VMEM((sections, 8, micros * pairs * tok), f32),
            pltpu.VMEM((8, micros * pairs * tok), f32),
            pltpu.VMEM((experts, 8, micros * pairs * tok), f32),
            dma((3,)),
            dma,
            dma,
            dma,
            dma,
            dma,
            dma((micros,)),
            dma((micros,)),
            dma((micros,)),
            dma((micros,)),
            dma((micros,)),
            dma((micros,)),
            dma((micros,)),
            dma((micros,)),
            dma((micros,)),
            dma((micros,)),
            dma((2,)),
            dma((2,)),
        ],
        compiler_params=pltpu.CompilerParams(
            collective_id=0, has_side_effects=True, vmem_limit_bytes=56 * 1024 * 1024
        ),
        name="relay",
    )(
        stream,
        layer_gain,
        router_weight[0],
        gate_weight[0, 0],
        up_weight[0, 0],
        down_weight[0, 0],
        routes[0],
        final_gain[None],
        head_weight,
        by_core,
    )
    loss = loss.reshape(2, micros, pairs, tok).transpose(1, 2, 0, 3)
    return loss.reshape(targets.shape)


def solution(mesh):
    in_specs = (
        P(None, "expert", "pipe"),
        P("pipe", None),
        P("pipe", None, None),
        P("pipe", "expert", None, None),
        P("pipe", "expert", None, None),
        P("pipe", "expert", None, None),
        P("pipe", None, "expert", None),
        P(),
        P(("pipe", "expert"), None),
        P(),
    )
    out_specs = P()
    return jax.shard_map(local, mesh=mesh, in_specs=in_specs, out_specs=out_specs, check_vma=False)
```

time: 1420 us -> 455 us (0.32)
  blocking collectives: 562 us -> 0 us
  waiting for transfers between devices: 511 us -> 0 us
  Pallas kernels: 0 us -> 447 us
  starting transfers between devices: 131 us -> 0 us
  matrix products: 123 us -> 0 us
  other arithmetic: 30.6 us -> 0 us
  local copies, waits for them, and re-layouts: 36.2 us -> 7.68 us
    all_gather x4 -> x0, blocking collectives: 562 us -> none  [the longest x3 522 us: merged(): gathered = jax.tree.map(lambda a: lax.all_gather(a, axis), part)]
    pallas_call x0 -> x1, Pallas kernels: none -> 447 us  [local(): pl.pallas_call(functools.partial(kernel, sections, experts), out_shape=ja...]
    all_to_all x18 -> x0, waiting for transfers between devices: 274 us -> none  [the longest x9 137 us: apply_layer(): lax.all_to_all(produced, 'expert', split_axis=0, concat_axis=0, tiled=True)]
    psum x1 -> x0, waiting for transfers between devices: 163 us -> none  [from_root(): return lax.psum(jnp.where(mine, array, jnp.zeros_like(array)), axis)]
    dot_general x37 -> x0, matrix products: 123 us -> none  [the longest x9 74.4 us: expert_work(): jnp.dot(hidden, w_down, preferred_element_type=jnp.float32)]
    all_to_all x18 -> x0, starting transfers between devices: 95.3 us -> none  [the longest x9 55.7 us: apply_layer(): lax.all_to_all(packed, 'expert', split_axis=0, concat_axis=0, tiled=True)]
    all_gather x1 -> x0, waiting for transfers between devices: 57.9 us -> none  [local(): collected_all = lax.all_gather(drafted, 'expert', axis=1, tiled=True)]
    ppermute x9 -> x0, starting transfers between devices: 35.4 us -> none  [shifted(): lax.ppermute(value, axis, [(source, source + steps) for source in range(l...]
  transfers between devices with their start and end apart: 29 -> 0, of which waited for: 29 -> 0; matrix products, arithmetic and copies ran while one was open for 1% -> 0% of each run, Pallas kernels for 0% -> 0%
where the time goes in v1:
time: 455 us
  Pallas kernels  447 us (98%)
  local copies, waits for them, and re-layouts  7.68 us (2%)
    pallas_call x1, Pallas kernels, local(): pl.pallas_call(functools.partial(kernel, sections, experts), out_shape=ja...  447 us

profile of v1, /device:TPU:1, one launch (start us, length us, event | category | flops | bytes accessed | tf_op | source)
XLA Modules:
  0.0 455.2 jit_solution(6614515937941217404)
XLA Ops:
  0.0 1.3 broadcast_in_dim.3.final_gain
  1.3 1.4 copy.12
  2.7 0.8 reshape.12
  3.5 0.7 reshape.13.targets
  4.1 2.1 copy.11
  6.3 447.5 %relay.1 = f32[2,256]{1,0:T(2,128)} custom-call(bf16[2,16,448]{2,1,0:T(8,128)(2,1)} %stream.1, f32[1,3584]{1,0:T(1,128)} %gain.1, bf16[3584,16]{1,0:T(8,128)(2,1)} %bitcast.14, bf16[3584,1024]{1,0:T(8,128)(2,1)} %bitcast.11, bf16[3584,1024]{1,0:T(8,128)(2,1)} %bitcast.12, bf16[1024,3584]{1,0:T(8,128)(2,1)} %bitcast.13, s32[2,16,8]{2,1,0:T(8,128)} %bitcast.17, ...), custom_call_target="tpu_custom_call" | custom-call | tf_op jit(solution)/shard_map/relay/pallas_call | solution.py:437
  453.8 0.7 reshape.14
  454.5 0.7 reshape.15
  (2 shorter events, 0.0 us)

commit v2 on v1

v2 whole, which is shorter than its diff:
```python
import functools

import jax
import jax.numpy as jnp
from jax import lax
from jax.experimental import pallas as pl
from jax.experimental.pallas import tpu as pltpu
from jax.sharding import PartitionSpec as P

routed_scale = 2.5
norm_eps = 1e-06
MESH = pl.DeviceIdType.MESH
f32 = jnp.float32
bf16 = jnp.bfloat16


def iota(shape, axis):
    return lax.broadcasted_iota(jnp.int32, shape, axis)


def dot(a, b):
    return jnp.dot(a, b, preferred_element_type=f32)


def dot_nt(a, b):
    return lax.dot_general(a, b, (((1,), (1,)), ((), ())), preferred_element_type=f32)


def dot_tn(a, b):
    return lax.dot_general(a, b, (((0,), (0,)), ((), ())), preferred_element_type=f32)


def kernel(
    sections,
    experts,
    stream,
    gain,
    router,
    w_gate,
    w_up,
    w_down,
    routes,
    final_gain,
    head,
    targets,
    loss,
    vg,
    vu,
    vd,
    vh,
    gath,
    xin,
    xcur,
    packed,
    recv,
    prod,
    ret,
    hidden,
    rows_in,
    rows_out,
    fin,
    dall,
    logits,
    spread,
    fold,
    fold_in,
    stat,
    stat_pipe,
    stat_mid,
    stat_all,
    w_sem,
    head_sem,
    head_send,
    head_recv,
    stream_send,
    stream_recv,
    disp_send,
    disp_recv,
    back_send,
    back_recv,
    hop_send,
    hop_recv,
    fold_send,
    fold_recv,
    fin_send,
    fin_recv,
    dall_send,
    dall_recv,
    stat_send,
    stat_recv,
):
    micros, tok, part = stream.shape
    half = xin.shape[2]
    width = 2 * half
    cap = 8
    block = 2 * cap
    pairs = experts // 2
    slots = experts * cap
    vdev = head.shape[0]
    p = lax.axis_index("pipe")
    e = lax.axis_index("expert")
    chip = e // 2
    core = lax.rem(e, 2)
    odd = lax.rem(p, 2)
    last = sections - 1

    def local(src, dst, sem):
        return pltpu.make_async_copy(src, dst, sem)

    def to(src, dst, send, recv_, device):
        return pltpu.make_async_remote_copy(
            src_ref=src, dst_ref=dst, send_sem=send, recv_sem=recv_, device_id=device, device_id_type=MESH
        )

    def drain(ref, sem):
        pltpu.make_async_copy(ref, ref, sem).wait()

    def other_expert(k):
        return lax.rem(e + k, experts)

    def other_section(k):
        return lax.rem(p + k, sections)

    def other_chip(k):
        return lax.rem(chip + k, pairs)

    def rows_of(index):
        return pl.ds(pl.multiple_of(index * block, block), block)

    def each(count, body, start=1):
        def step(k, carry):
            body(k)
            return carry

        lax.fori_loop(start, count, step, 0)

    weights = [
        local(w_gate, vg, w_sem.at[0]),
        local(w_up, vu, w_sem.at[1]),
        local(w_down, vd, w_sem.at[2]),
    ]
    for copy in weights:
        copy.start()
    own_head = local(head, vh.at[core], head_sem)
    own_head.start()

    barrier = pltpu.get_barrier_semaphore()

    def greet(device):
        pl.semaphore_signal(barrier, inc=1, device_id=device, device_id_type=MESH)

    partner = p + 1 - 2 * odd
    each(sections, lambda k: greet((other_section(k), e)))
    each(experts, lambda k: greet((p, other_expert(k))))
    each(experts, lambda k: greet((partner, other_expert(k))))
    pl.semaphore_wait(barrier, 2 * (experts - 1) + sections - 1)

    stream_out = to(stream, gath.at[p], stream_send, stream_recv, (0, e))

    @pl.when(p > 0)
    def _():
        stream_out.start()

    @pl.when(p == 0)
    def _():
        local(stream, gath.at[0], stream_recv).start()

    head_out = to(head, vh.at[core], head_send, head_recv, (p, 2 * chip + 1 - core))
    head_out.start()

    expert_of = (iota((experts, 2 * slots), 1) // block == iota((experts, 2 * slots), 0)).astype(bf16)
    expert_of_t = (iota((2 * slots, experts), 0) // block == iota((2 * slots, experts), 1)).astype(bf16)
    earlier = (iota((tok, tok), 0) < iota((tok, tok), 1)).astype(bf16)

    def tables(m):
        route = routes[m]
        member = jnp.zeros((experts, tok), f32)
        for k in range(route.shape[0]):
            member = member + (route[k : k + 1, :] == iota((experts, tok), 0)).astype(f32)
        place = dot(member.astype(bf16), earlier)
        code = jnp.where(member > 0, place, -1.0).astype(bf16)
        return member, code

    for m in range(micros):
        member, code = tables(m)
        chosen = dot(expert_of_t, code)
        row = iota((2 * slots, tok), 0)
        valid = chosen == lax.rem(row, cap).astype(f32)
        side = lax.rem(row // cap, 2)
        spread[m] = jnp.concatenate(
            [(valid & (side == 0)).astype(bf16), (valid & (side == 1)).astype(bf16)], axis=1
        )

    gather_row = iota((slots, slots), 0)
    gather_col = iota((slots, slots), 1)

    def interleaved(index):
        side = index // (slots // 2)
        source = lax.rem(index, slots // 2) // cap
        return source * block + side * cap + lax.rem(index, cap)

    apart = (interleaved(gather_row) == gather_col).astype(bf16)
    together = (interleaved(gather_col) == gather_row).astype(bf16)

    @pl.when(p == 0)
    def _():
        drain(gath, stream_recv)
        per = sections // 2
        for m in range(micros):
            for side in range(2):
                for j in range(per):
                    xin[m, side * tok : (side + 1) * tok, j * part : (j + 1) * part] = gath[side * per + j, m]

    def normed_of(value, first_gain, second_gain):
        wide = value.astype(f32)
        square = jnp.sum(wide * wide, axis=1, keepdims=True)
        mean = (square[:tok] + square[tok:]) / width
        inverse = lax.rsqrt(mean + norm_eps)
        first = wide[:tok] * inverse * first_gain
        second = wide[tok:] * inverse * second_gain
        return jnp.concatenate([first, second], axis=0).astype(bf16)

    def mixed(value, weights_, blocks):
        out = dot(weights_, blocks)
        return (value.astype(f32) + out[: 2 * tok] + out[2 * tok :]).astype(bf16)

    def dispatch(m):
        @pl.when(p > 0)
        def _():
            drain(xin.at[m], hop_recv.at[m])

        @pl.when(odd == 1)
        def _():
            drain(fold_in.at[m], fold_recv.at[m])
            drain(ret.at[0, m], back_recv.at[0, m])
            xcur[m] = mixed(xin[m], fold_in[m], ret[0, m])

        @pl.when(odd == 0)
        def _():
            xcur[m] = xin[m]

        normed = normed_of(xcur[m], gain[:, :half], gain[:, half:])
        packed[m] = dot(spread[m], normed).astype(bf16)

        def send(k):
            peer = other_expert(k)
            to(
                packed.at[m, rows_of(peer)],
                recv.at[m, core, rows_of(chip)],
                disp_send.at[m],
                disp_recv.at[m, core],
                (p, peer),
            ).start()

        each(experts, send)
        local(packed.at[m, rows_of(e)], recv.at[m, core, rows_of(chip)], disp_recv.at[m, core]).start()
        member, code = tables(m)
        affinity = dot_nt(router[:, :half], normed[:tok]) + dot_nt(router[:, half:], normed[tok:])
        affinity = jax.nn.sigmoid(affinity) * member
        weight = routed_scale * affinity / jnp.sum(affinity, axis=0, keepdims=True)
        upper = weight.astype(bf16)
        lower = (weight - upper.astype(f32)).astype(bf16)
        chosen = dot_tn(code, expert_of)
        column = iota((tok, 2 * slots), 1)
        valid = chosen == lax.rem(column, cap).astype(f32)
        side = lax.rem(column // cap, 2)
        upper = dot_tn(upper, expert_of)
        lower = dot_tn(lower, expert_of)
        one = valid & (side == 0)
        two = valid & (side == 1)
        fold[m] = jnp.concatenate(
            [jnp.where(one, upper, 0.0), jnp.where(two, upper, 0.0), jnp.where(one, lower, 0.0), jnp.where(two, lower, 0.0)],
            axis=0,
        ).astype(bf16)

        @pl.when(odd == 0)
        def _():
            to(xin.at[m], xin.at[m], hop_send.at[m], hop_recv.at[m], (p + 1, e)).start()
            to(fold.at[m], fold_in.at[m], fold_send.at[m], fold_recv.at[m], (p + 1, e)).start()

    def expert_work(m, c):
        drain(recv.at[m, c], disp_recv.at[m, c])
        if m == 0 and c == 0:
            weights[0].wait()
            weights[1].wait()
        rows_in[...] = dot(apart, recv[m, c]).astype(bf16)
        rows = slots // 2
        tile = min(512, hidden.shape[1])

        def up(n, carry):
            cols = pl.ds(pl.multiple_of(n * tile, tile), tile)
            gated = dot(rows_in[:rows], vg[:half, cols]) + dot(rows_in[rows:], vg[half:, cols])
            lifted = dot(rows_in[:rows], vu[:half, cols]) + dot(rows_in[rows:], vu[half:, cols])
            hidden[:, cols] = (gated / (1.0 + jnp.exp(-gated)) * lifted).astype(bf16)
            return carry

        lax.fori_loop(0, hidden.shape[1] // tile, up, 0)
        if m == 0 and c == 0:
            weights[2].wait()
        step = min(256, half)

        def down(n, carry):
            first = pl.ds(pl.multiple_of(n * step, 128), step)
            second = pl.ds(pl.multiple_of(half + n * step, 128), step)
            rows_out[:rows, first] = dot(hidden[...], vd[:, first]).astype(bf16)
            rows_out[rows:, first] = dot(hidden[...], vd[:, second]).astype(bf16)
            return carry

        lax.fori_loop(0, half // step, down, 0)
        prod[m, c] = dot(together, rows_out[...]).astype(bf16)

        def send(k):
            peer = other_chip(k)
            to(
                prod.at[m, c, rows_of(peer)],
                ret.at[odd, m, rows_of(e)],
                back_send.at[m, c],
                back_recv.at[odd, m],
                (p + 1 - odd, 2 * peer + c),
            ).start()

        each(pairs, send)
        here = (odd == 1) & (core == c)

        @pl.when(here)
        def _():
            local(prod.at[m, c, rows_of(chip)], ret.at[1, m, rows_of(e)], back_recv.at[1, m]).start()

        @pl.when(jnp.logical_not(here))
        def _():
            send(0)

    def share(m):
        def send(k):
            peer = 2 * other_chip(k) + core
            to(fin.at[m], dall.at[m, chip], dall_send.at[m], dall_recv.at[m], (p, peer)).start()

        each(pairs, send)
        local(fin.at[m], dall.at[m, chip], dall_recv.at[m]).start()

    def combine(m):
        drain(ret.at[1, m], back_recv.at[1, m])
        out = mixed(xcur[m], fold[m], ret[1, m])

        @pl.when(p < last)
        def _():
            xcur[m] = out
            to(xcur.at[m], xin.at[m], hop_send.at[m], hop_recv.at[m], (p + 1, e)).start()

        @pl.when(p == last)
        def _():
            fin[m] = normed_of(out, final_gain[:half][None], final_gain[half:][None])

            def send(k):
                to(fin.at[m], fin.at[m], fin_send.at[m], fin_recv.at[m], (other_section(k), e)).start()

            each(sections, send)
            share(m)

    def arrive(m):
        @pl.when(p < last)
        def _():
            drain(fin.at[m], fin_recv.at[m])
            share(m)

    def head_work(m):
        drain(dall.at[m], dall_recv.at[m])
        if m == 0:
            own_head.wait()
            head_out.wait()
        states = dall[m].reshape(pairs, 2, tok, half)
        first = states[:, 0].reshape(pairs * tok, half)
        second = states[:, 1].reshape(pairs * tok, half)
        tile = min(256, vdev)
        per = vdev // tile

        def step(n, carry):
            part_ = vh.at[n // per]
            rows = pl.ds(pl.multiple_of(lax.rem(n, per) * tile, tile), tile)
            value = dot_nt(part_[rows, :half], first) + dot_nt(part_[rows, half:], second)
            logits[pl.ds(pl.multiple_of(n * tile, tile), tile)] = value
            return carry

        lax.fori_loop(0, 2 * per, step, 0)
        value = logits[...]
        highest = jnp.max(value, axis=0, keepdims=True)
        total = jnp.sum(jnp.exp(value - highest), axis=0, keepdims=True)
        count = experts * tok
        lane = iota((count, pairs * tok), 1)
        pick = (iota((count, pairs * tok), 0) == (2 * (lane // tok) + core) * tok + lax.rem(lane, tok)).astype(bf16)
        wanted = targets[m : m + 1, :]
        upper = wanted // 256
        lower = wanted - upper * 256
        wanted = 256.0 * dot(upper.astype(f32).astype(bf16), pick) + dot(lower.astype(f32).astype(bf16), pick)
        entry = iota(value.shape, 0) + (p * experts + 2 * chip) * vdev
        hit = jnp.sum(jnp.where(entry.astype(f32) == wanted, value, 0.0), axis=0, keepdims=True)
        stat[:, m * pairs * tok : (m + 1) * pairs * tok] = jnp.concatenate(
            [highest, total, hit, jnp.zeros((5, pairs * tok), f32)], axis=0
        )

    @pl.when(core == 0)
    def _():
        dispatch(0)

    expert_work(0, 0)

    @pl.when(core == 1)
    def _():
        dispatch(0)

    @pl.when((core == 0) & (odd == 1))
    def _():
        combine(0)

    expert_work(0, 1)

    @pl.when(core == 0)
    def _():
        dispatch(1)

    @pl.when((core == 1) & (odd == 1))
    def _():
        combine(0)

    expert_work(1, 0)

    @pl.when(core == 1)
    def _():
        dispatch(1)

    @pl.when((core == 0) & (odd == 1))
    def _():
        combine(1)

    expert_work(1, 1)

    @pl.when((core == 1) & (odd == 1))
    def _():
        combine(1)


    arrive(0)
    head_work(0)
    arrive(1)
    head_work(1)

    def merged(parts):
        highest = functools.reduce(jnp.maximum, [part_[0:1] for part_ in parts])
        total = sum(part_[1:2] * jnp.exp(part_[0:1] - highest) for part_ in parts)
        hit = sum(part_[2:3] for part_ in parts)
        return highest, total, hit

    def send_pipe(k):
        to(stat, stat_pipe.at[p], stat_send.at[0], stat_recv.at[0], (other_section(k), e)).start()

    each(sections, send_pipe)
    local(stat, stat_pipe.at[p], stat_recv.at[0]).start()
    drain(stat_pipe, stat_recv.at[0])
    highest, total, hit = merged([stat_pipe[j] for j in range(sections)])
    stat_mid[...] = jnp.concatenate([highest, total, hit, jnp.zeros((5, highest.shape[1]), f32)], axis=0)

    def send_all(k):
        to(stat_mid, stat_all.at[e], stat_send.at[1], stat_recv.at[1], (p, other_expert(k))).start()

    each(experts, send_all)
    local(stat_mid, stat_all.at[e], stat_recv.at[1]).start()
    drain(stat_all, stat_recv.at[1])
    count = experts * tok
    result = jnp.zeros((micros, count), f32)
    for c in range(2):
        highest, total, hit = merged([stat_all[2 * j + c] for j in range(pairs)])
        value = highest + jnp.log(total) - hit
        value = jnp.concatenate([value[:, m * pairs * tok : (m + 1) * pairs * tok] for m in range(micros)], axis=0)
        lane = iota((pairs * tok, count), 0)
        pick = ((2 * (lane // tok) + c) * tok + lax.rem(lane, tok) == iota((pairs * tok, count), 1)).astype(bf16)
        for _ in range(3):
            piece = value.astype(bf16)
            value = value - piece.astype(f32)
            result = result + dot(piece, pick)
    loss[...] = result

    @pl.when(p > 0)
    def _():
        drain(stream, stream_send)

    for m in range(micros):
        drain(packed.at[m, pl.ds(0, 2 * slots - block)], disp_send.at[m])
        for c in range(2):
            drain(prod.at[m, c, pl.ds(0, slots - block)], back_send.at[m, c])

            @pl.when(jnp.logical_not((odd == 1) & (core == c)))
            def _():
                drain(prod.at[m, c, pl.ds(0, block)], back_send.at[m, c])

        @pl.when(p < last)
        def _():
            drain(xin.at[m], hop_send.at[m])

        @pl.when(odd == 0)
        def _():
            drain(fold.at[m], fold_send.at[m])

        @pl.when(p == last)
        def _():
            for _ in range(sections - 1):
                drain(fin.at[m], fin_send.at[m])

        drain(dall.at[m, pl.ds(0, pairs - 1)], dall_send.at[m])
    drain(stat_pipe.at[pl.ds(0, sections - 1)], stat_send.at[0])
    drain(stat_all.at[pl.ds(0, experts - 1)], stat_send.at[1])


def local(
    stream,
    layer_gain,
    router_weight,
    gate_weight,
    up_weight,
    down_weight,
    routes,
    final_gain,
    head_weight,
    targets,
):
    sections = lax.axis_size("pipe")
    experts = lax.axis_size("expert")
    micros, tok, part = stream.shape
    width = layer_gain.shape[1]
    half = width // 2
    hidden = gate_weight.shape[3]
    vdev = head_weight.shape[0]
    pairs = experts // 2
    slots = experts * 8
    dma = pltpu.SemaphoreType.DMA
    vmem = pl.BlockSpec(memory_space=pltpu.VMEM)
    hbm = pl.BlockSpec(memory_space=pl.ANY)
    return pl.pallas_call(
        functools.partial(kernel, sections, experts),
        out_shape=jax.ShapeDtypeStruct(targets.shape, f32),
        in_specs=[hbm, vmem, vmem, hbm, hbm, hbm, vmem, vmem, hbm, vmem],
        out_specs=vmem,
        scratch_shapes=[
            pltpu.VMEM((width, hidden), bf16),
            pltpu.VMEM((width, hidden), bf16),
            pltpu.VMEM((hidden, width), bf16),
            pltpu.VMEM((2, vdev, width), bf16),
            pltpu.VMEM((sections, micros, tok, part), bf16),
            pltpu.VMEM((micros, 2 * tok, half), bf16),
            pltpu.VMEM((micros, 2 * tok, half), bf16),
            pltpu.VMEM((micros, 2 * slots, half), bf16),
            pltpu.VMEM((micros, 2, slots, half), bf16),
            pltpu.VMEM((micros, 2, slots, half), bf16),
            pltpu.VMEM((2, micros, 2 * slots, half), bf16),
            pltpu.VMEM((slots // 2, hidden), bf16),
            pltpu.VMEM((slots, half), bf16),
            pltpu.VMEM((slots, half), bf16),
            pltpu.VMEM((micros, 2 * tok, half), bf16),
            pltpu.VMEM((micros, pairs, 2 * tok, half), bf16),
            pltpu.VMEM((2 * vdev, pairs * tok), f32),
            pltpu.VMEM((micros, 2 * slots, 2 * tok), bf16),
            pltpu.VMEM((micros, 4 * tok, 2 * slots), bf16),
            pltpu.VMEM((micros, 4 * tok, 2 * slots), bf16),
            pltpu.VMEM((8, micros * pairs * tok), f32),
            pltpu.VMEM((sections, 8, micros * pairs * tok), f32),
            pltpu.VMEM((8, micros * pairs * tok), f32),
            pltpu.VMEM((experts, 8, micros * pairs * tok), f32),
            dma((3,)),
            dma,
            dma,
            dma,
            dma,
            dma,
            dma((micros,)),
            dma((micros, 2)),
            dma((micros, 2)),
            dma((2, micros)),
            dma((micros,)),
            dma((micros,)),
            dma((micros,)),
            dma((micros,)),
            dma((micros,)),
            dma((micros,)),
            dma((micros,)),
            dma((micros,)),
            dma((2,)),
            dma((2,)),
        ],
        compiler_params=pltpu.CompilerParams(
            collective_id=0, has_side_effects=True, vmem_limit_bytes=56 * 1024 * 1024
        ),
        name="relay",
    )(
        stream,
        layer_gain,
        router_weight[0].T,
        gate_weight[0, 0],
        up_weight[0, 0],
        down_weight[0, 0],
        jnp.swapaxes(routes[0], 1, 2),
        final_gain,
        head_weight,
        targets,
    )


def solution(mesh):
    in_specs = (
        P(None, "expert", "pipe"),
        P("pipe", None),
        P("pipe", None, None),
        P("pipe", "expert", None, None),
        P("pipe", "expert", None, None),
        P("pipe", "expert", None, None),
        P("pipe", None, "expert", None),
        P(),
        P(("pipe", "expert"), None),
        P(),
    )
    out_specs = P()
    return jax.shard_map(local, mesh=mesh, in_specs=in_specs, out_specs=out_specs, check_vma=False)
```

time: 455 us -> 323 us (0.71)
  Pallas kernels: 447 us -> 322 us
  local copies, waits for them, and re-layouts: 7.68 us -> 1.26 us
    pallas_call x1, Pallas kernels: 447 us -> 322 us  [local(): pl.pallas_call(functools.partial(kernel, sections, experts), out_shape=ja...]
where the time goes in v2:
time: 323 us
  Pallas kernels  322 us (100%)
    pallas_call x1, Pallas kernels, local(): pl.pallas_call(functools.partial(kernel, sections, experts), out_shape=ja...  322 us

profile of v2, /device:TPU:1, one launch (start us, length us, event | category | flops | bytes accessed | tf_op | source)
XLA Modules:
  0.0 323.0 jit_solution(9505144124956075993)
XLA Ops:
  0.0 321.7 %relay.1 = f32[2,256]{1,0:T(2,128)} custom-call(bf16[2,16,448]{2,1,0:T(8,128)(2,1)} %stream.1, f32[1,3584]{1,0:T(1,128)} %gain.1, bf16[16,3584]{1,0:T(8,128)(2,1)} %bitcast.12, bf16[3584,1024]{1,0:T(8,128)(2,1)} %bitcast.9, bf16[3584,1024]{1,0:T(8,128)(2,1)} %bitcast.10, bf16[1024,3584]{1,0:T(8,128)(2,1)} %bitcast.11, s32[2,8,16]{2,1,0:T(8,128)} %bitcast.13, ...), custom_call_target="tpu_custom_call" | custom-call | tf_op jit(solution)/shard_map/relay/pallas_call | solution.py:537
  321.7 1.3 copy.12

commit v3 on v2

--- a/solution.py
+++ b/solution.py
@@ -56,8 +56,7 @@
     prod,
     ret,
     hidden,
-    rows_in,
-    rows_out,
+    partial,
     fin,
     dall,
     logits,
@@ -86,6 +85,7 @@
     fin_recv,
     dall_send,
     dall_recv,
+    relay_send,
     stat_send,
     stat_recv,
 ):
@@ -103,6 +103,11 @@
     core = lax.rem(e, 2)
     odd = lax.rem(p, 2)
     last = sections - 1
+    lead = (half * 4 // 7 + 255) // 256 * 256 if half > 512 else half // 2
+    pieces = [pl.ds(0, lead), pl.ds(lead, half - lead)]
+
+    def shifted(piece):
+        return pl.ds(half + piece.start, piece.size)
 
     def local(src, dst, sem):
         return pltpu.make_async_copy(src, dst, sem)
@@ -232,28 +237,33 @@
         @pl.when(odd == 1)
         def _():
             drain(fold_in.at[m], fold_recv.at[m])
-            drain(ret.at[0, m], back_recv.at[0, m])
-            xcur[m] = mixed(xin[m], fold_in[m], ret[0, m])
+            for q, cols in enumerate(pieces):
+                drain(ret.at[0, m, :, cols], back_recv.at[q, 0, m])
+                xcur[m, :, cols] = mixed(xin[m, :, cols], fold_in[m], ret[0, m, :, cols])
 
         @pl.when(odd == 0)
         def _():
             xcur[m] = xin[m]
 
         normed = normed_of(xcur[m], gain[:, :half], gain[:, half:])
-        packed[m] = dot(spread[m], normed).astype(bf16)
-
-        def send(k):
-            peer = other_expert(k)
-            to(
-                packed.at[m, rows_of(peer)],
-                recv.at[m, core, rows_of(chip)],
-                disp_send.at[m],
-                disp_recv.at[m, core],
-                (p, peer),
+        for q, cols in enumerate(pieces):
+            packed[m, :, cols] = dot(spread[m], normed[:, cols.start : cols.start + cols.size]).astype(bf16)
+
+            def send(k, q=q, cols=cols):
+                peer = other_expert(k)
+                to(
+                    packed.at[m, rows_of(peer), cols],
+                    recv.at[m, core, rows_of(chip), cols],
+                    disp_send.at[m],
+                    disp_recv.at[q, m, core],
+                    (p, peer),
+                ).start()
+
+            each(experts, send)
+            local(
+                packed.at[m, rows_of(e), cols], recv.at[m, core, rows_of(chip), cols], disp_recv.at[q, m, core]
             ).start()
 
-        each(experts, send)
-        local(packed.at[m, rows_of(e)], recv.at[m, core, rows_of(chip)], disp_recv.at[m, core]).start()
         member, code = tables(m)
         affinity = dot_nt(router[:, :half], normed[:tok]) + dot_nt(router[:, half:], normed[tok:])
         affinity = jax.nn.sigmoid(affinity) * member
@@ -279,56 +289,63 @@
             to(fold.at[m], fold_in.at[m], fold_send.at[m], fold_recv.at[m], (p + 1, e)).start()
 
     def expert_work(m, c):
-        drain(recv.at[m, c], disp_recv.at[m, c])
-        if m == 0 and c == 0:
-            weights[0].wait()
-            weights[1].wait()
-        rows_in[...] = dot(apart, recv[m, c]).astype(bf16)
         rows = slots // 2
         tile = min(512, hidden.shape[1])
-
-        def up(n, carry):
-            cols = pl.ds(pl.multiple_of(n * tile, tile), tile)
-            gated = dot(rows_in[:rows], vg[:half, cols]) + dot(rows_in[rows:], vg[half:, cols])
-            lifted = dot(rows_in[:rows], vu[:half, cols]) + dot(rows_in[rows:], vu[half:, cols])
-            hidden[:, cols] = (gated / (1.0 + jnp.exp(-gated)) * lifted).astype(bf16)
-            return carry
-
-        lax.fori_loop(0, hidden.shape[1] // tile, up, 0)
-        if m == 0 and c == 0:
+        for q, cols in enumerate(pieces):
+            drain(recv.at[m, c, :, cols], disp_recv.at[q, m, c])
+            if q == 0:
+
+                @pl.when((m == 0) & (c == 0))
+                def _():
+                    weights[0].wait()
+                    weights[1].wait()
+
+            given = dot(apart, recv[m, c, :, cols]).astype(bf16)
+            second = shifted(cols)
+            for n in range(hidden.shape[1] // tile):
+                part_ = pl.ds(n * tile, tile)
+                gated = dot(given[:rows], vg[cols, part_]) + dot(given[rows:], vg[second, part_])
+                lifted = dot(given[:rows], vu[cols, part_]) + dot(given[rows:], vu[second, part_])
+                if q == 0:
+                    partial[0, :, part_] = gated
+                    partial[1, :, part_] = lifted
+                else:
+                    gated = gated + partial[0, :, part_]
+                    lifted = lifted + partial[1, :, part_]
+                    hidden[:, part_] = (gated / (1.0 + jnp.exp(-gated)) * lifted).astype(bf16)
+
+        @pl.when((m == 0) & (c == 0))
+        def _():
             weights[2].wait()
-        step = min(256, half)
-
-        def down(n, carry):
-            first = pl.ds(pl.multiple_of(n * step, 128), step)
-            second = pl.ds(pl.multiple_of(half + n * step, 128), step)
-            rows_out[:rows, first] = dot(hidden[...], vd[:, first]).astype(bf16)
-            rows_out[rows:, first] = dot(hidden[...], vd[:, second]).astype(bf16)
-            return carry
-
-        lax.fori_loop(0, half // step, down, 0)
-        prod[m, c] = dot(together, rows_out[...]).astype(bf16)
-
-        def send(k):
-            peer = other_chip(k)
-            to(
-                prod.at[m, c, rows_of(peer)],
-                ret.at[odd, m, rows_of(e)],
-                back_send.at[m, c],
-                back_recv.at[odd, m],
-                (p + 1 - odd, 2 * peer + c),
-            ).start()
-
-        each(pairs, send)
+
         here = (odd == 1) & (core == c)
-
-        @pl.when(here)
-        def _():
-            local(prod.at[m, c, rows_of(chip)], ret.at[1, m, rows_of(e)], back_recv.at[1, m]).start()
-
-        @pl.when(jnp.logical_not(here))
-        def _():
-            send(0)
+        for q, cols in enumerate(pieces):
+            out = jnp.concatenate(
+                [dot(hidden[...], vd[:, cols]).astype(bf16), dot(hidden[...], vd[:, shifted(cols)]).astype(bf16)], axis=0
+            )
+            prod[m, c, :, cols] = dot(together, out).astype(bf16)
+
+            def send(k, q=q, cols=cols):
+                peer = other_chip(k)
+                to(
+                    prod.at[m, c, rows_of(peer), cols],
+                    ret.at[odd, m, rows_of(e), cols],
+                    back_send.at[m, c],
+                    back_recv.at[q, odd, m],
+                    (p + 1 - odd, 2 * peer + c),
+                ).start()
+
+            each(pairs, send)
+
+            @pl.when(here)
+            def _(q=q, cols=cols):
+                local(
+                    prod.at[m, c, rows_of(chip), cols], ret.at[1, m, rows_of(e), cols], back_recv.at[q, 1, m]
+                ).start()
+
+            @pl.when(jnp.logical_not(here))
+            def _(send=send):
+                send(0)
 
     def share(m):
         def send(k):
@@ -339,35 +356,54 @@
         local(fin.at[m], dall.at[m, chip], dall_recv.at[m]).start()
 
     def combine(m):
-        drain(ret.at[1, m], back_recv.at[1, m])
-        out = mixed(xcur[m], fold[m], ret[1, m])
-
-        @pl.when(p < last)
-        def _():
-            xcur[m] = out
-            to(xcur.at[m], xin.at[m], hop_send.at[m], hop_recv.at[m], (p + 1, e)).start()
+        for q, cols in enumerate(pieces):
+            drain(ret.at[1, m, :, cols], back_recv.at[q, 1, m])
+            xcur[m, :, cols] = mixed(xcur[m, :, cols], fold[m], ret[1, m, :, cols])
+
+            @pl.when(p < last)
+            def _(cols=cols):
+                to(
+                    xcur.at[m, :, cols], xin.at[m, :, cols], hop_send.at[m], hop_recv.at[m], (p + 1, e)
+                ).start()
 
         @pl.when(p == last)
         def _():
-            fin[m] = normed_of(out, final_gain[:half][None], final_gain[half:][None])
+            fin[m] = normed_of(xcur[m], final_gain[:half][None], final_gain[half:][None])
 
             def send(k):
                 to(fin.at[m], fin.at[m], fin_send.at[m], fin_recv.at[m], (other_section(k), e)).start()
 
             each(sections, send)
+
+            @pl.when((m == micros - 1) & (core == 1))
+            def _():
+                share(m)
+
+    def arrive(m):
+        drain(fin.at[m], fin_recv.at[m])
+
+        @pl.when((p < last - 1) | ((m == micros - 1) & (core == 1)))
+        def _():
             share(m)
 
-    def arrive(m):
-        @pl.when(p < last)
-        def _():
-            drain(fin.at[m], fin_recv.at[m])
-            share(m)
+    def relayed(m):
+        return (p >= last - 3) & (p < last - 1) & jnp.logical_not((m == micros - 1) & (core == 1))
+
+    def relay_out(m):
+        return to(dall.at[m], dall.at[m], relay_send.at[m], dall_recv.at[m], (p + 2, e))
 
     def head_work(m):
         drain(dall.at[m], dall_recv.at[m])
-        if m == 0:
+
+        @pl.when(relayed(m))
+        def _():
+            relay_out(m).start()
+
+        @pl.when(m == 0)
+        def _():
             own_head.wait()
             head_out.wait()
+
         states = dall[m].reshape(pairs, 2, tok, half)
         first = states[:, 0].reshape(pairs * tok, half)
         second = states[:, 1].reshape(pairs * tok, half)
@@ -388,66 +424,48 @@
         count = experts * tok
         lane = iota((count, pairs * tok), 1)
         pick = (iota((count, pairs * tok), 0) == (2 * (lane // tok) + core) * tok + lax.rem(lane, tok)).astype(bf16)
-        wanted = targets[m : m + 1, :]
+        wanted = targets[pl.ds(m, 1), :]
         upper = wanted // 256
         lower = wanted - upper * 256
         wanted = 256.0 * dot(upper.astype(f32).astype(bf16), pick) + dot(lower.astype(f32).astype(bf16), pick)
         entry = iota(value.shape, 0) + (p * experts + 2 * chip) * vdev
         hit = jnp.sum(jnp.where(entry.astype(f32) == wanted, value, 0.0), axis=0, keepdims=True)
-        stat[:, m * pairs * tok : (m + 1) * pairs * tok] = jnp.concatenate(
+        stat[m] = jnp.concatenate(
             [highest, total, hit, jnp.zeros((5, pairs * tok), f32)], axis=0
         )
 
-    @pl.when(core == 0)
-    def _():
-        dispatch(0)
-
-    expert_work(0, 0)
-
-    @pl.when(core == 1)
-    def _():
-        dispatch(0)
-
-    @pl.when((core == 0) & (odd == 1))
-    def _():
-        combine(0)
-
-    expert_work(0, 1)
-
-    @pl.when(core == 0)
-    def _():
-        dispatch(1)
-
-    @pl.when((core == 1) & (odd == 1))
-    def _():
-        combine(0)
-
-    expert_work(1, 0)
-
-    @pl.when(core == 1)
-    def _():
-        dispatch(1)
-
-    @pl.when((core == 0) & (odd == 1))
-    def _():
-        combine(1)
-
-    expert_work(1, 1)
-
-    @pl.when((core == 1) & (odd == 1))
-    def _():
-        combine(1)
-
-
-    arrive(0)
-    head_work(0)
-    arrive(1)
-    head_work(1)
+    def chunk(j, carry):
+        m = j // 2
+        c = lax.rem(j, 2)
+
+        @pl.when(core == c)
+        def _():
+            dispatch(m)
+
+        expert_work(m, c)
+
+        @pl.when((core == c) & (odd == 1))
+        def _():
+            combine(m)
+
+        return carry
+
+    lax.fori_loop(0, 2 * micros, chunk, 0)
+
+    def draft(m, carry):
+        @pl.when(p < last)
+        def _():
+            arrive(m)
+
+        head_work(m)
+        return carry
+
+    lax.fori_loop(0, micros, draft, 0)
 
     def merged(parts):
-        highest = functools.reduce(jnp.maximum, [part_[0:1] for part_ in parts])
-        total = sum(part_[1:2] * jnp.exp(part_[0:1] - highest) for part_ in parts)
-        hit = sum(part_[2:3] for part_ in parts)
+        highest = functools.reduce(jnp.maximum, [part_[:, 0:1] for part_ in parts])
+        total = sum(part_[:, 1:2] * jnp.exp(part_[:, 0:1] - highest) for part_ in parts)
+        hit = sum(part_[:, 2:3] for part_ in parts)
         return highest, total, hit
 
     def send_pipe(k):
@@ -457,7 +475,7 @@
     local(stat, stat_pipe.at[p], stat_recv.at[0]).start()
     drain(stat_pipe, stat_recv.at[0])
     highest, total, hit = merged([stat_pipe[j] for j in range(sections)])
-    stat_mid[...] = jnp.concatenate([highest, total, hit, jnp.zeros((5, highest.shape[1]), f32)], axis=0)
+    stat_mid[...] = jnp.concatenate([highest, total, hit, jnp.zeros((micros, 5, pairs * tok), f32)], axis=1)
 
     def send_all(k):
         to(stat_mid, stat_all.at[e], stat_send.at[1], stat_recv.at[1], (p, other_expert(k))).start()
@@ -470,7 +488,7 @@
     for c in range(2):
         highest, total, hit = merged([stat_all[2 * j + c] for j in range(pairs)])
         value = highest + jnp.log(total) - hit
-        value = jnp.concatenate([value[:, m * pairs * tok : (m + 1) * pairs * tok] for m in range(micros)], axis=0)
+        value = jnp.concatenate([value[m] for m in range(micros)], axis=0)
         lane = iota((pairs * tok, count), 0)
         pick = ((2 * (lane // tok) + c) * tok + lax.rem(lane, tok) == iota((pairs * tok, count), 1)).astype(bf16)
         for _ in range(3):
@@ -505,7 +523,14 @@
             for _ in range(sections - 1):
                 drain(fin.at[m], fin_send.at[m])
 
-        drain(dall.at[m, pl.ds(0, pairs - 1)], dall_send.at[m])
+        @pl.when((p < last - 1) | ((m == micros - 1) & (core == 1)))
+        def _():
+            drain(dall.at[m, pl.ds(0, pairs - 1)], dall_send.at[m])
+
+        @pl.when(relayed(m))
+        def _():
+            drain(dall.at[m], relay_send.at[m])
+
     drain(stat_pipe.at[pl.ds(0, sections - 1)], stat_send.at[0])
     drain(stat_all.at[pl.ds(0, experts - 1)], stat_send.at[1])
 
@@ -552,18 +577,17 @@
             pltpu.VMEM((micros, 2, slots, half), bf16),
             pltpu.VMEM((2, micros, 2 * slots, half), bf16),
             pltpu.VMEM((slots // 2, hidden), bf16),
-            pltpu.VMEM((slots, half), bf16),
-            pltpu.VMEM((slots, half), bf16),
+            pltpu.VMEM((2, slots // 2, hidden), f32),
             pltpu.VMEM((micros, 2 * tok, half), bf16),
             pltpu.VMEM((micros, pairs, 2 * tok, half), bf16),
             pltpu.VMEM((2 * vdev, pairs * tok), f32),
             pltpu.VMEM((micros, 2 * slots, 2 * tok), bf16),
             pltpu.VMEM((micros, 4 * tok, 2 * slots), bf16),
             pltpu.VMEM((micros, 4 * tok, 2 * slots), bf16),
-            pltpu.VMEM((8, micros * pairs * tok), f32),
-            pltpu.VMEM((sections, 8, micros * pairs * tok), f32),
-            pltpu.VMEM((8, micros * pairs * tok), f32),
-            pltpu.VMEM((experts, 8, micros * pairs * tok), f32),
+            pltpu.VMEM((micros, 8, pairs * tok), f32),
+            pltpu.VMEM((sections, micros, 8, pairs * tok), f32),
+            pltpu.VMEM((micros, 8, pairs * tok), f32),
+            pltpu.VMEM((experts, micros, 8, pairs * tok), f32),
             dma((3,)),
             dma,
             dma,
@@ -571,9 +595,10 @@
             dma,
             dma,
             dma((micros,)),
+            dma((2, micros, 2)),
             dma((micros, 2)),
-            dma((micros, 2)),
-            dma((2, micros)),
+            dma((2, 2, micros)),
+            dma((micros,)),
             dma((micros,)),
             dma((micros,)),
             dma((micros,)),

time: 323 us -> 298 us (0.923)
  Pallas kernels: 322 us -> 296 us
    pallas_call x1, Pallas kernels: 322 us -> 296 us  [local(): pl.pallas_call(functools.partial(kernel, sections, experts), out_shape=ja...]
where the time goes in v3:
time: 298 us
  Pallas kernels  296 us (99%)
    pallas_call x1, Pallas kernels, local(): pl.pallas_call(functools.partial(kernel, sections, experts), out_shape=ja...  296 us

profile of v3, /device:TPU:1, one launch (start us, length us, event | category | flops | bytes accessed | tf_op | source)
XLA Modules:
  0.0 297.7 jit_solution(15062630857689226338)
XLA Ops:
  0.0 296.4 %relay.1 = f32[2,256]{1,0:T(2,128)} custom-call(bf16[2,16,448]{2,1,0:T(8,128)(2,1)} %stream.1, f32[1,3584]{1,0:T(1,128)} %gain.1, bf16[16,3584]{1,0:T(8,128)(2,1)} %bitcast.12, bf16[3584,1024]{1,0:T(8,128)(2,1)} %bitcast.9, bf16[3584,1024]{1,0:T(8,128)(2,1)} %bitcast.10, bf16[1024,3584]{1,0:T(8,128)(2,1)} %bitcast.11, s32[2,8,16]{2,1,0:T(8,128)} %bitcast.13, ...), custom_call_target="tpu_custom_call" | custom-call | tf_op jit(solution)/shard_map/relay/pallas_call | solution.py:562
  296.4 1.3 copy.12

commit v4 on v3

--- a/solution.py
+++ b/solution.py
@@ -196,17 +196,6 @@
             [(valid & (side == 0)).astype(bf16), (valid & (side == 1)).astype(bf16)], axis=1
         )
 
-    gather_row = iota((slots, slots), 0)
-    gather_col = iota((slots, slots), 1)
-
-    def interleaved(index):
-        side = index // (slots // 2)
-        source = lax.rem(index, slots // 2) // cap
-        return source * block + side * cap + lax.rem(index, cap)
-
-    apart = (interleaved(gather_row) == gather_col).astype(bf16)
-    together = (interleaved(gather_col) == gather_row).astype(bf16)
-
     @pl.when(p == 0)
     def _():
         drain(gath, stream_recv)
@@ -300,12 +289,14 @@
                     weights[0].wait()
                     weights[1].wait()
 
-            given = dot(apart, recv[m, c, :, cols]).astype(bf16)
+            blocks = recv[m, c, :, cols].astype(f32).reshape(pairs, 2, cap, cols.size)
+            one = blocks[:, 0].reshape(rows, cols.size).astype(bf16)
+            two = blocks[:, 1].reshape(rows, cols.size).astype(bf16)
             second = shifted(cols)
             for n in range(hidden.shape[1] // tile):
                 part_ = pl.ds(n * tile, tile)
-                gated = dot(given[:rows], vg[cols, part_]) + dot(given[rows:], vg[second, part_])
-                lifted = dot(given[:rows], vu[cols, part_]) + dot(given[rows:], vu[second, part_])
+                gated = dot(one, vg[cols, part_]) + dot(two, vg[second, part_])
+                lifted = dot(one, vu[cols, part_]) + dot(two, vu[second, part_])
                 if q == 0:
                     partial[0, :, part_] = gated
                     partial[1, :, part_] = lifted
@@ -320,10 +311,9 @@
 
         here = (odd == 1) & (core == c)
         for q, cols in enumerate(pieces):
-            out = jnp.concatenate(
-                [dot(hidden[...], vd[:, cols]).astype(bf16), dot(hidden[...], vd[:, shifted(cols)]).astype(bf16)], axis=0
-            )
-            prod[m, c, :, cols] = dot(together, out).astype(bf16)
+            one = dot(hidden[...], vd[:, cols]).reshape(pairs, cap, cols.size)
+            two = dot(hidden[...], vd[:, shifted(cols)]).reshape(pairs, cap, cols.size)
+            prod[m, c, :, cols] = jnp.concatenate([one, two], axis=1).reshape(slots, cols.size).astype(bf16)
 
             def send(k, q=q, cols=cols):
                 peer = other_chip(k)

time: 298 us -> 294 us (0.987)
  Pallas kernels: 296 us -> 293 us
    pallas_call x1, Pallas kernels: 296 us -> 293 us  [local(): pl.pallas_call(functools.partial(kernel, sections, experts), out_shape=ja...]
where the time goes in v4:
time: 294 us
  Pallas kernels  293 us (100%)
    pallas_call x1, Pallas kernels, local(): pl.pallas_call(functools.partial(kernel, sections, experts), out_shape=ja...  293 us

profile of v4, /device:TPU:1, one launch (start us, length us, event | category | flops | bytes accessed | tf_op | source)
XLA Modules:
  0.0 293.9 jit_solution(6845954550077250706)
XLA Ops:
  0.0 292.6 %relay.1 = f32[2,256]{1,0:T(2,128)} custom-call(bf16[2,16,448]{2,1,0:T(8,128)(2,1)} %stream.1, f32[1,3584]{1,0:T(1,128)} %gain.1, bf16[16,3584]{1,0:T(8,128)(2,1)} %bitcast.12, bf16[3584,1024]{1,0:T(8,128)(2,1)} %bitcast.9, bf16[3584,1024]{1,0:T(8,128)(2,1)} %bitcast.10, bf16[1024,3584]{1,0:T(8,128)(2,1)} %bitcast.11, s32[2,8,16]{2,1,0:T(8,128)} %bitcast.13, ...), custom_call_target="tpu_custom_call" | custom-call | tf_op jit(solution)/shard_map/relay/pallas_call | solution.py:552
  292.6 1.3 copy.12
